TPU v7x, 32 devices: a whole 2x2x4 slice. The times are simulated.
32 devices in a mesh: dp: 4 (over z), seq: 2 (over y), tensor: 4 (over x, core).
Axes of the slice: x: 2, y: 2, z: 4, core: 2. Of those that a mesh axis runs over, the one named last changes fastest.
Arguments:
- block_input: float32 [8192, 768], P(('dp', 'seq', 'tensor')), may hold values from -6 to 6
- attn_in_weight: bfloat16 [3, 768, 768], P(None, ('dp', 'seq'), 'tensor'), may hold values from -0.21875 to 0.21875
- attn_out_weight: bfloat16 [768, 768], P('tensor', ('dp', 'seq')), may hold values from -3.5 to 3.5
- position_bias: float32 [32, 12], P(None, 'tensor'), may hold values from -6 to 6
- norm_gains: float32 [2, 768], replicated, may hold values from 0.1 to 1.9
- router_weight: bfloat16 [768, 8], replicated, may hold values from -0.15625 to 0.15625
- expert_in: bfloat16 [8, 768, 3072], P(('dp', 'seq'), None, 'tensor'), may hold values from -0.21875 to 0.21875
- expert_out: bfloat16 [8, 3072, 768], P(('dp', 'seq'), 'tensor'), may hold values from -10 to 10
- segment_ids: int32 [4, 2048], P('dp', ('seq', 'tensor')), may hold values from 0 to 2, as said below
- expert_ids: int32 [8192, 1], P(('dp', 'seq')), may hold values from 0 to 7; in each aligned block of 1024 rows (0 to 1023, 1024 to 2047, ...) at most 256 rows name the same one
- out_grad: float32 [8192, 768], P(('dp', 'seq', 'tensor')), may hold values from -6 to 6
Outputs:
- block_out: float32 [8192, 768], P(('dp', 'seq', 'tensor'))
- input_grad: float32 [8192, 768], P(('dp', 'seq', 'tensor'))
- grad_attn_in: float32 [3, 768, 768], P(None, ('dp', 'seq'), 'tensor')
- grad_attn_out: float32 [768, 768], P('tensor', ('dp', 'seq'))
- grad_bias: float32 [32, 12], P(None, 'tensor')
- grad_gains: float32 [2, 768], replicated
- grad_router: float32 [768, 8], replicated
- grad_expert_in: float32 [8, 768, 3072], P(('dp', 'seq'), None, 'tensor')
- grad_expert_out: float32 [8, 3072, 768], P(('dp', 'seq'), 'tensor')
Inputs may be any that keep to these rules, and one draw needn't show every extreme that they name: `segment_ids`: along a sequence the ids never fall; every sequence holds documents 0, 1 and 2, each one run of positions. In some sequence document 1 begins within the first 1024 positions and ends within the last 1024. `expert_ids`: in each aligned block of 1024 rows no expert is named by more than 256 rows.
All inputs are finite; a program needn't handle non-finite values.
Results may differ from a plain program's by a relative error of at most 0.035.
Values may be sent and summed in bfloat16 or wider, within the bound.
No kernel may reach another device: no remote copies, remote signals or barrier semaphores. Data moves between devices by JAX's collectives and lax.ppermute only.
A program may use at most 448 MiB of HBM per device.

v0:
```python
import functools
import math

import jax
import jax.numpy as jnp
from jax import lax
from jax.experimental import pallas as pl
from jax.experimental.pallas import tpu as pltpu
from jax.sharding import PartitionSpec as P

EPSILON = 1e-06
EDGES = (1, 2, 3, 4, 5, 6, 7, 8, 12, 16, 23, 32, 46, 64, 91)
TILE = 256
HALF = TILE // 2
LOG2E = math.log2(math.e)
SCALE = 0.125
MASKED = -1e30
LOWEST = -1e29
VMEM_BYTES = 48 * 1024 * 1024
GELU_A = math.sqrt(2.0 / math.pi)
GELU_B = 0.044715
BF16 = jnp.bfloat16
F32 = jnp.float32


def dot(left_side, right_side):
    return jnp.dot(left_side, right_side, preferred_element_type=F32)


def dot_rows(left_side, right_side):
    return lax.dot_general(
        left_side, right_side, (((1,), (1,)), ((), ())), preferred_element_type=F32
    )


def einsum(formula, *operands):
    return jnp.einsum(formula, *operands, preferred_element_type=F32)


def swap(values, axis, bit):
    count = lax.axis_size(axis)
    return lax.ppermute(values, axis, [(i, i ^ bit) for i in range(count)])


def bits_of(count):
    return [1 << i for i in range(count.bit_length() - 1)]


def gather_relative(values, axis):
    pieces = {0: values}
    for bit in reversed(bits_of(lax.axis_size(axis))):
        for place in list(pieces):
            pieces[place ^ bit] = swap(pieces[place], axis, bit)
    return [pieces[place] for place in range(len(pieces))]


def sum_relative(kept, sent, axis):
    total = kept.astype(F32) + swap(sent.astype(BF16), axis, 1).astype(F32)
    bit = 2
    while bit < lax.axis_size(axis):
        pairs = total.reshape((-1, 2) + total.shape[1:])
        total = pairs[:, 0] + swap(pairs[:, 1].astype(BF16), axis, bit).astype(F32)
        bit *= 2
    return total[0]


def reorder(pieces, own_index):
    for bit in bits_of(len(pieces)):
        flip = (own_index & bit) != 0
        pieces = [
            jnp.where(flip, pieces[place ^ bit], pieces[place]) for place in range(len(pieces))
        ]
    return pieces


def gather_grid(values):
    dp_count, seq_count = lax.axis_size("dp"), lax.axis_size("seq")
    if dp_count > 4 or seq_count != 2:
        return lax.all_gather(values, ("dp", "seq"), axis=0, tiled=False)
    columns = [values] + [swap(values, "dp", place) for place in range(1, dp_count)]
    near = swap(values, "seq", 1)
    far = swap(jnp.stack(columns[1:]), "seq", 1)
    pieces = [values, near]
    for place in range(1, dp_count):
        pieces += [columns[place], far[place - 1]]
    own = lax.axis_index("dp") * seq_count + lax.axis_index("seq")
    return jnp.stack(reorder(pieces, own))


def scatter_grid(blocks):
    dp_count, seq_count = lax.axis_size("dp"), lax.axis_size("seq")
    if dp_count > 4 or seq_count != 2:
        return lax.psum_scatter(
            blocks.astype(BF16), ("dp", "seq"), scatter_dimension=0, tiled=False
        ).astype(F32)
    own = lax.axis_index("dp") * seq_count + lax.axis_index("seq")
    parts = reorder([blocks[place] for place in range(dp_count * seq_count)], own)
    sent = swap(jnp.stack(parts[1::2]).astype(BF16), "seq", 1)
    parts = [parts[2 * place] + sent[place].astype(F32) for place in range(dp_count)]
    total = parts[0]
    for place in range(1, dp_count):
        total = total + swap(parts[place].astype(BF16), "dp", place).astype(F32)
    return total


def sum_all(values, axes):
    for axis in axes:
        for bit in bits_of(lax.axis_size(axis)):
            values = values + swap(values, axis, bit)
    return values


def bucket_of(relative, half_count):
    magnitude = jnp.abs(relative)
    counted = jnp.zeros(relative.shape, jnp.int32)
    for edge_value in EDGES:
        counted = counted + (magnitude >= edge_value).astype(jnp.int32)
    return counted + jnp.where(relative > 0, half_count, 0).astype(jnp.int32)


def near_buckets(half_count):
    shape = (3, HALF, HALF)
    relative = (
        (lax.broadcasted_iota(jnp.int32, shape, 0) - 1) * HALF
        + lax.broadcasted_iota(jnp.int32, shape, 1)
        - lax.broadcasted_iota(jnp.int32, shape, 2)
    )
    return bucket_of(relative, half_count)


def bias_tiles(position_bias):
    bucket_count, heads = position_bias.shape
    half_count = bucket_count // 2
    grid = near_buckets(half_count)
    near = jnp.zeros((heads, 3, HALF, HALF), F32)
    for bucket_index in range(bucket_count):
        near = near + jnp.where(
            (grid == bucket_index)[None], position_bias[bucket_index][:, None, None, None], 0.0
        )
    before, same, after = near[:, 0], near[:, 1], near[:, 2]
    far_before = jnp.broadcast_to(
        position_bias[half_count - 1][:, None, None], (heads, HALF, HALF)
    )
    far_after = jnp.broadcast_to(
        position_bias[bucket_count - 1][:, None, None], (heads, HALF, HALF)
    )

    def square(a, b, c, d):
        return jnp.concatenate(
            [jnp.concatenate([a, b], axis=2), jnp.concatenate([c, d], axis=2)], axis=1
        )

    tiles = jnp.stack(
        [
            square(far_before, far_before, far_before, far_before),
            square(far_before, far_before, before, far_before),
            square(same, before, after, same),
            square(far_after, after, far_after, far_after),
            square(far_after, far_after, far_after, far_after),
        ]
    )
    return tiles * LOG2E


def bias_sums(tiles, bucket_count):
    half_count = bucket_count // 2
    first, last = slice(0, HALF), slice(HALF, TILE)
    same = tiles[2][:, first, first] + tiles[2][:, last, last]
    before = tiles[2][:, first, last] + tiles[1][:, last, first]
    after = tiles[2][:, last, first] + tiles[3][:, first, last]
    near = jnp.stack([before, same, after], axis=1)
    grid = near_buckets(half_count)
    rows = [
        jnp.sum(jnp.where((grid == bucket_index)[None], near, 0.0), axis=(1, 2, 3))
        for bucket_index in range(bucket_count)
    ]
    rows[half_count - 1] = (
        rows[half_count - 1]
        + jnp.sum(tiles[0], axis=(1, 2))
        + jnp.sum(tiles[1][:, first, :], axis=(1, 2))
        + jnp.sum(tiles[1][:, last, last], axis=(1, 2))
    )
    rows[bucket_count - 1] = (
        rows[bucket_count - 1]
        + jnp.sum(tiles[4], axis=(1, 2))
        + jnp.sum(tiles[3][:, last, :], axis=(1, 2))
        + jnp.sum(tiles[3][:, first, first], axis=(1, 2))
    )
    return jnp.stack(rows)


def span_of(meta_ref, query_tile, key_tiles):
    opening, closing = meta_ref[1], meta_ref[2]
    first = query_tile * TILE
    last = first + TILE - 1
    begin = jnp.where(first < opening, 0, jnp.where(first < closing, opening, closing))
    end = jnp.where(last < opening, opening, jnp.where(last < closing, closing, key_tiles * TILE))
    return begin // TILE, (end + TILE - 1) // TILE


def document_of(meta_ref, tile, dimension):
    place = tile * TILE + lax.broadcasted_iota(jnp.int32, (TILE, TILE), dimension)
    return (place >= meta_ref[1]).astype(jnp.int32) + (place >= meta_ref[2]).astype(jnp.int32)


def attend_kernel(meta_ref, q_ref, kv_ref, bias_ref, exact_ref, out_ref, log_ref, key_ref, sum_ref):
    key_tiles = kv_ref.shape[0]
    heads = bias_ref.shape[1]
    size = q_ref.shape[1] // heads

    def turn(tile, carry):
        for h in range(heads):
            key_ref[tile, h] = kv_ref[tile, h * size : (h + 1) * size, :].T
        return carry

    lax.fori_loop(0, key_tiles, turn, 0)

    def query_body(i, carry):
        tile = meta_ref[3 + key_tiles + i]
        place = tile % meta_ref[0]
        begin, end = span_of(meta_ref, tile, key_tiles)
        own_document = document_of(meta_ref, tile, 1)
        sum_ref[...] = jnp.zeros_like(sum_ref)

        def key_body(j, stats):
            allowed = document_of(meta_ref, j, 0) == own_document
            kind = jnp.clip(j - tile, -2, 2) + 2
            stats = list(stats)
            kept = meta_ref[3 + j]
            for h in range(heads):
                peak, total = stats[2 * h], stats[2 * h + 1]
                rows = slice(h * size, (h + 1) * size)
                scores = dot(key_ref[kept, h], q_ref[i, rows, :]) * LOG2E + bias_ref[kind, h]
                scores = jnp.where(allowed, scores, MASKED)
                new_peak = jnp.maximum(peak, jnp.max(scores, axis=0, keepdims=True))
                faded = jnp.exp2(peak - new_peak)
                weights = jnp.exp2(scores - new_peak)
                stats[2 * h] = new_peak
                stats[2 * h + 1] = total * faded + jnp.sum(weights, axis=0, keepdims=True)
                values = kv_ref[kept, (heads + h) * size : (heads + h + 1) * size, :]
                sum_ref[rows, :] = sum_ref[rows, :] * faded + dot(values, weights.astype(BF16))
            return tuple(stats)

        start = []
        for h in range(heads):
            start += [jnp.full((1, TILE), LOWEST, F32), jnp.zeros((1, TILE), F32)]
        stats = lax.fori_loop(begin, end, key_body, tuple(start))
        for h in range(heads):
            rows = slice(h * size, (h + 1) * size)
            result = sum_ref[rows, :] * (1.0 / stats[2 * h + 1])
            exact_ref[i, rows, :] = result
            out_ref[place, rows, :] = result.astype(BF16)
            log_ref[i, h] = stats[2 * h] + jnp.log2(stats[2 * h + 1])
        return carry

    lax.fori_loop(0, q_ref.shape[0], query_body, 0)


def estimate(queries, key_tiles, products):
    pairs = queries.shape[0] * TILE * key_tiles * TILE
    return pl.CostEstimate(
        flops=2 * products * pairs * queries.shape[1],
        bytes_accessed=8 * pairs,
        transcendentals=3 * pairs,
    )


def whole_specs(count):
    return [pl.BlockSpec(memory_space=pltpu.VMEM)] * count


def attend(meta, queries, keys_values, bias):
    query_tiles, width, _ = queries.shape
    key_tiles = keys_values.shape[0]
    heads = bias.shape[1]
    return pl.pallas_call(
        attend_kernel,
        out_shape=(
            jax.ShapeDtypeStruct(queries.shape, F32),
            jax.ShapeDtypeStruct(queries.shape, BF16),
            jax.ShapeDtypeStruct((query_tiles, heads, 1, TILE), F32),
        ),
        in_specs=[pl.BlockSpec(memory_space=pltpu.SMEM)] + whole_specs(3),
        out_specs=tuple(whole_specs(3)),
        scratch_shapes=[
            pltpu.VMEM((key_tiles, heads, TILE, width // heads), BF16),
            pltpu.VMEM((width, TILE), F32),
        ],
        compiler_params=pltpu.CompilerParams(vmem_limit_bytes=VMEM_BYTES),
        cost_estimate=estimate(queries, key_tiles, 2),
        name="attend",
    )(meta, queries, keys_values, bias)


def attend_back_kernel(
    meta_ref,
    q_ref,
    kv_ref,
    bias_ref,
    grad_ref,
    exact_ref,
    log_ref,
    dq_ref,
    dkv_ref,
    tiles_ref,
    key_ref,
    value_ref,
    dq_sum,
    dkv_sum,
):
    key_tiles = kv_ref.shape[0]
    heads = bias_ref.shape[1]
    size = q_ref.shape[1] // heads

    def turn(tile, carry):
        for h in range(heads):
            key_ref[tile, h] = kv_ref[tile, h * size : (h + 1) * size, :].T
            value_ref[tile, h] = kv_ref[tile, (heads + h) * size : (heads + h + 1) * size, :].T
        return carry

    lax.fori_loop(0, key_tiles, turn, 0)
    dkv_sum[...] = jnp.zeros_like(dkv_sum)
    tiles_ref[...] = jnp.zeros_like(tiles_ref)

    def query_body(i, carry):
        tile = meta_ref[3 + key_tiles + i]
        place = tile % meta_ref[0]
        begin, end = span_of(meta_ref, tile, key_tiles)
        own_document = document_of(meta_ref, tile, 1)
        dq_sum[...] = jnp.zeros_like(dq_sum)
        centres = []
        for h in range(heads):
            rows = slice(h * size, (h + 1) * size)
            centres.append(
                jnp.sum(grad_ref[place, rows, :].astype(F32) * exact_ref[i, rows, :], axis=0, keepdims=True)
            )

        def key_body(j, inner):
            allowed = document_of(meta_ref, j, 0) == own_document
            kept = meta_ref[3 + j]
            kind = jnp.clip(j - tile, -2, 2) + 2
            for h in range(heads):
                rows = slice(h * size, (h + 1) * size)
                value_rows = slice((heads + h) * size, (heads + h + 1) * size)
                query = q_ref[i, rows, :]
                grad = grad_ref[place, rows, :]
                scores = dot(key_ref[kept, h], query) * LOG2E + bias_ref[kind, h]
                probs = jnp.where(allowed, jnp.exp2(scores - log_ref[i, h]), 0.0)
                prob_grad = dot(value_ref[kept, h], grad)
                score_grad = probs * (prob_grad - centres[h])
                tiles_ref[kind, h] += score_grad
                low_grad = score_grad.astype(BF16)
                dkv_sum[kept, rows, :] += dot_rows(query, low_grad)
                dkv_sum[kept, value_rows, :] += dot_rows(grad, probs.astype(BF16))
                dq_sum[rows, :] += dot(kv_ref[kept, rows, :], low_grad)
            return inner

        lax.fori_loop(begin, end, key_body, 0)
        dq_ref[i] = (dq_sum[...] * SCALE).astype(BF16)
        return carry

    lax.fori_loop(0, q_ref.shape[0], query_body, 0)
    dkv_ref[...] = dkv_sum[...].astype(BF16)


def attend_back(meta, queries, keys_values, bias, grad, exact, logs):
    key_tiles = keys_values.shape[0]
    heads = bias.shape[1]
    size = queries.shape[1] // heads
    return pl.pallas_call(
        attend_back_kernel,
        out_shape=(
            jax.ShapeDtypeStruct(queries.shape, BF16),
            jax.ShapeDtypeStruct(keys_values.shape, BF16),
            jax.ShapeDtypeStruct(bias.shape, F32),
        ),
        in_specs=[pl.BlockSpec(memory_space=pltpu.SMEM)] + whole_specs(6),
        out_specs=tuple(whole_specs(3)),
        scratch_shapes=[
            pltpu.VMEM((key_tiles, heads, TILE, size), BF16),
            pltpu.VMEM((key_tiles, heads, TILE, size), BF16),
            pltpu.VMEM(queries.shape[1:], F32),
            pltpu.VMEM(keys_values.shape, F32),
        ],
        compiler_params=pltpu.CompilerParams(vmem_limit_bytes=VMEM_BYTES),
        cost_estimate=estimate(queries, key_tiles, 5),
        name="attend_back",
    )(meta, queries, keys_values, bias, grad, exact, logs)


def split_low(values):
    high = values.astype(BF16)
    return high, (values - high.astype(F32)).astype(BF16)


def load_tile(ref, *place):
    return jnp.concatenate([ref[(m, *place)] for m in range(ref.shape[0])], axis=-1)


def expert_kernel(
    parts,
    own_ref,
    *refs,
):
    state_refs = refs[:parts]
    (grad_ref, other_ref, in_ref, in_t_ref, out_ref, router_ref, router_t_ref, gain_ref) = refs[
        parts : parts + 8
    ]
    (
        kept_ref,
        sent_ref,
        normed_ref,
        full_ref,
        act_ref,
        pre_ref,
        gate_ref,
        gain_sum,
        router_sum,
        state_ref,
        back_ref,
    ) = refs[parts + 8 :]

    @pl.when(pl.program_id(0) == 0)
    def _():
        gain_sum[...] = jnp.zeros_like(gain_sum)
        router_sum[...] = jnp.zeros_like(router_sum)

    width = gain_ref.shape[0]
    share = width // parts
    expert, own = own_ref[0], own_ref[1]
    for k in range(parts):
        state_ref[own ^ k] = load_tile(state_refs[k])
        full_ref[0, own ^ k] = load_tile(other_ref if k & 1 else grad_ref, k // 2)
    columns = state_ref.shape[-1]
    state = state_ref[...].reshape(width, columns).astype(F32)
    root = lax.rsqrt(jnp.sum(state * state, axis=0, keepdims=True) * (1.0 / width) + EPSILON)
    gain = gain_ref[...]
    normed = (state * root * gain).astype(BF16)
    normed_ref[0] = normed
    logits = dot(router_t_ref[...], normed)
    raised = jnp.exp(logits - jnp.max(logits, axis=0, keepdims=True))
    router_probs = raised / jnp.sum(raised, axis=0, keepdims=True)
    chosen = lax.broadcasted_iota(jnp.int32, logits.shape, 0) == expert
    gate = jnp.sum(jnp.where(chosen, router_probs, 0.0), axis=0, keepdims=True)
    gate_ref[0] = gate
    act_grad = dot(out_ref[...], full_ref[0].reshape(width, columns))
    pre_act = dot(in_t_ref[...], normed)
    square = pre_act * pre_act
    bent = jnp.tanh(GELU_A * pre_act * (1.0 + GELU_B * square))
    cdf = 0.5 + 0.5 * bent
    activated = (pre_act * cdf).astype(BF16)
    act_ref[0] = activated
    slope = cdf + (0.5 * GELU_A) * pre_act * (1.0 - bent * bent) * (1.0 + (3.0 * GELU_B) * square)
    pre_grad = (act_grad * gate * slope).astype(BF16)
    pre_ref[0] = pre_grad
    gate_grad = jnp.sum(activated.astype(F32) * act_grad, axis=0, keepdims=True)
    logit_grad = gate_grad * gate * (chosen.astype(F32) - router_probs)
    high, low = split_low(logit_grad)
    router = router_ref[...]
    normed_grad = dot(in_ref[...], pre_grad) + dot(router, high) + dot(router, low)
    router_sum[...] += dot_rows(high, normed) + dot_rows(low, normed)
    plain = normed.astype(F32)
    product = normed_grad * plain
    gain_sum[...] += product
    centre = jnp.sum(product, axis=0, keepdims=True) * (1.0 / width)
    back = root * (normed_grad * gain - plain * (centre * (1.0 / gain)))
    back_ref[...] = back.astype(BF16).reshape(parts, share, columns)
    merged = kept_ref.shape[1]
    slots = columns // merged
    for k in range(parts):
        block = back_ref[own ^ k]
        target = sent_ref if k & 1 else kept_ref
        for m in range(merged):
            target[k // 2, m] = block[:, m * slots : (m + 1) * slots]


def result_kernel(parts, own_ref, *refs):
    chunks = (len(refs) - 7) // 5
    sets = [refs[5 * c : 5 * c + 5] for c in range(chunks)]
    out_t_ref, kept_ref, sent_ref, in_sum, out_sum, result_ref, _ = refs[5 * chunks :]

    @pl.when(pl.program_id(0) == 0)
    def _():
        in_sum[...] = jnp.zeros_like(in_sum)
        out_sum[...] = jnp.zeros_like(out_sum)

    own = own_ref[1]
    width = out_t_ref.shape[0]
    share = width // parts
    for c in range(chunks):
        normed_ref, full_ref, act_ref, pre_ref, gate_ref = sets[c]
        gate, activated = gate_ref[0], act_ref[0]
        columns = activated.shape[-1]
        in_sum[...] += dot_rows(normed_ref[0], pre_ref[0])
        scaled = (full_ref[0].reshape(width, columns).astype(F32) * gate).astype(BF16)
        out_sum[...] += dot_rows(activated, scaled)
        result = dot(out_t_ref[...], activated) * gate
        result_ref[...] = result.astype(BF16).reshape(parts, share, columns)
        merged = kept_ref.shape[1]
        slots = columns // merged
        for k in range(parts):
            block = result_ref[own ^ k]
            target = sent_ref if k & 1 else kept_ref
            for m in range(merged):
                target[k // 2, m, :, c * slots : (c + 1) * slots] = block[
                    :, m * slots : (m + 1) * slots
                ]


def fixed_spec(shape):
    return pl.BlockSpec(shape, lambda g: (0,) * len(shape))


def run_expert(own, states, grads, chunk, merged, weights):
    parts = len(states)
    count, share, slots = states[0].shape
    width = share * parts
    columns = merged * slots
    steps = count // merged
    hidden = weights[0].shape[1]
    experts = weights[3].shape[1]
    half = parts // 2
    piece = pl.BlockSpec((merged, share, slots), lambda g: (g, 0, 0))
    grad_piece = pl.BlockSpec((merged, half, share, slots), lambda g: (g, 0, 0, chunk))
    split = pl.BlockSpec((half, merged, share, slots), lambda g: (0, g, 0, 0))
    wide = pl.BlockSpec((1, width, columns), lambda g: (g, 0, 0))
    deep = pl.BlockSpec((1, hidden, columns), lambda g: (g, 0, 0))
    tall = pl.BlockSpec((1, parts, share, columns), lambda g: (g, 0, 0, 0))
    flat = pl.BlockSpec((1, 1, columns), lambda g: (g, 0, 0))
    return pl.pallas_call(
        functools.partial(expert_kernel, parts),
        grid=(steps,),
        out_shape=(
            jax.ShapeDtypeStruct((half, count, share, slots), BF16),
            jax.ShapeDtypeStruct((half, count, share, slots), BF16),
            jax.ShapeDtypeStruct((steps, width, columns), BF16),
            jax.ShapeDtypeStruct((steps, parts, share, columns), BF16),
            jax.ShapeDtypeStruct((steps, hidden, columns), BF16),
            jax.ShapeDtypeStruct((steps, hidden, columns), BF16),
            jax.ShapeDtypeStruct((steps, 1, columns), F32),
            jax.ShapeDtypeStruct((width, columns), F32),
            jax.ShapeDtypeStruct((experts, width), F32),
        ),
        in_specs=[pl.BlockSpec(memory_space=pltpu.SMEM)]
        + [piece] * parts
        + [grad_piece] * 2
        + [fixed_spec(weight.shape) for weight in weights],
        out_specs=(
            split,
            split,
            wide,
            tall,
            deep,
            deep,
            flat,
            fixed_spec((width, columns)),
            fixed_spec((experts, width)),
        ),
        scratch_shapes=[
            pltpu.VMEM((parts, share, columns), BF16),
            pltpu.VMEM((parts, share, columns), BF16),
        ],
        compiler_params=pltpu.CompilerParams(vmem_limit_bytes=VMEM_BYTES),
        cost_estimate=pl.CostEstimate(
            flops=6 * steps * columns * width * hidden,
            bytes_accessed=16 * steps * columns * width,
            transcendentals=steps * columns * hidden,
        ),
        name="expert",
    )(own, *states, *grads, *weights)


def run_result(own, saved, merged, out_t):
    chunks = len(saved)
    steps, parts, share, columns = saved[0][1].shape
    width = parts * share
    hidden = saved[0][2].shape[1]
    slots = columns // merged
    half = parts // 2
    wide = pl.BlockSpec((1, width, columns), lambda g: (g, 0, 0))
    deep = pl.BlockSpec((1, hidden, columns), lambda g: (g, 0, 0))
    tall = pl.BlockSpec((1, parts, share, columns), lambda g: (g, 0, 0, 0))
    flat = pl.BlockSpec((1, 1, columns), lambda g: (g, 0, 0))
    split = pl.BlockSpec((half, merged, share, slots * chunks), lambda g: (0, g, 0, 0))
    total = jax.ShapeDtypeStruct((half, steps * merged, share, slots * chunks), BF16)
    return pl.pallas_call(
        functools.partial(result_kernel, parts),
        grid=(steps,),
        out_shape=(
            total,
            total,
            jax.ShapeDtypeStruct((width, hidden), F32),
            jax.ShapeDtypeStruct((hidden, width), F32),
        ),
        in_specs=[pl.BlockSpec(memory_space=pltpu.SMEM)]
        + [wide, tall, deep, deep, flat] * chunks
        + [fixed_spec(out_t.shape)],
        out_specs=(split, split, fixed_spec((width, hidden)), fixed_spec((hidden, width))),
        scratch_shapes=[
            pltpu.VMEM((parts, share, columns), BF16),
            pltpu.SMEM((1,), jnp.int32),
        ],
        compiler_params=pltpu.CompilerParams(vmem_limit_bytes=VMEM_BYTES),
        cost_estimate=pl.CostEstimate(
            flops=6 * chunks * steps * columns * width * hidden,
            bytes_accessed=12 * chunks * steps * columns * width,
            transcendentals=0,
        ),
        name="result",
    )(own, *[array for arrays in saved for array in arrays], out_t)


def norm_back(values, gain_row, grad):
    root = lax.rsqrt(jnp.mean(values * values, axis=-1, keepdims=True) + EPSILON)
    scaled = grad * gain_row
    return root * scaled - values * root**3 * jnp.mean(scaled * values, axis=-1, keepdims=True)


def shards(
    block_input,
    attn_in_weight,
    attn_out_weight,
    position_bias,
    norm_gains,
    router_weight,
    expert_in,
    expert_out,
    segment_ids,
    expert_ids,
    out_grad,
):
    tensor_count, seq_count = lax.axis_size("tensor"), lax.axis_size("seq")
    tensor_place, seq_place = lax.axis_index("tensor"), lax.axis_index("seq")
    grid_place = lax.axis_index("dp") * seq_count + seq_place
    local_count, width = block_input.shape
    group_count = local_count * tensor_count
    share = width // tensor_count
    bucket_count, heads = position_bias.shape
    head_cols = attn_in_weight.shape[2]
    experts = router_weight.shape[1]
    capacity = max(2, 2 * group_count // experts)
    tiles = group_count // TILE
    key_tiles = tiles * seq_count
    fast = seq_count == 2 and local_count == TILE

    def relative(values, axis=0):
        shape = values.shape
        blocks = values.reshape(
            shape[:axis] + (tensor_count, shape[axis] // tensor_count) + shape[axis + 1 :]
        )
        return [
            lax.dynamic_index_in_dim(blocks, tensor_place ^ k, axis, keepdims=False)
            for k in range(tensor_count)
        ]

    id_row = jnp.pad(segment_ids.astype(BF16), ((0, 15), (0, width - local_count)))
    own_rows = jnp.concatenate([block_input.astype(BF16), id_row])
    if seq_count == 2:
        both_rows = jnp.stack([own_rows, swap(own_rows, "seq", 1)])
    else:
        both_rows = lax.all_gather(own_rows, "seq", axis=0, tiled=False)
    row_pieces = gather_relative(both_rows, "tensor")
    weight_pieces = jnp.concatenate(
        [jnp.transpose(attn_in_weight, (1, 0, 2)), jnp.transpose(attn_out_weight)[:, None]], axis=1
    )
    weights_full = gather_grid(weight_pieces).reshape(width, 4, head_cols)
    in_full, out_full = weights_full[:, :3], weights_full[:, 3]
    all_ids = jnp.stack([piece[:, local_count, :local_count] for piece in row_pieces])
    opening = jnp.sum((all_ids < 0.5).astype(jnp.int32))
    closing = jnp.sum((all_ids < 1.5).astype(jnp.int32))
    slots_of_keys = jnp.arange(key_tiles, dtype=jnp.int32)
    tile_of_queries = seq_place * tiles + jnp.arange(tiles, dtype=jnp.int32)
    if fast:
        input_tiles = jnp.stack(
            [piece[s, :local_count] for s in range(seq_count) for piece in row_pieces]
        )
        slots_of_keys = ((slots_of_keys // tiles) ^ seq_place) * tiles + (
            (slots_of_keys % tiles) ^ tensor_place
        )
        tile_of_queries = seq_place * tiles + (
            jnp.arange(tiles, dtype=jnp.int32) ^ tensor_place
        )
        own_tiles = input_tiles[:tiles]
    else:
        ordered = reorder([piece[:, :local_count] for piece in row_pieces], tensor_place)
        ordered = jnp.stack(ordered, axis=1).reshape(seq_count, group_count, width)
        if seq_count == 2:
            ordered = jnp.stack(reorder([ordered[0], ordered[1]], seq_place))
        input_tiles = ordered.reshape(key_tiles, TILE, width)
        own_tiles = lax.dynamic_slice_in_dim(input_tiles, seq_place * tiles, tiles, 0)
    meta = jnp.concatenate(
        [
            jnp.stack([jnp.int32(tiles), opening, closing]),
            slots_of_keys.astype(jnp.int32),
            tile_of_queries.astype(jnp.int32),
        ]
    )
    bias = bias_tiles(position_bias)

    def normed_of(rows):
        wide_rows = rows.astype(F32)
        root = lax.rsqrt(jnp.mean(wide_rows * wide_rows, axis=-1, keepdims=True) + EPSILON)
        return (wide_rows * root * norm_gains[0]).astype(BF16)

    normed_tiles = normed_of(input_tiles)
    own_normed = normed_tiles[:tiles] if fast else normed_of(own_tiles)

    route_all = expert_ids[:, 0]
    expert_range = jnp.arange(experts, dtype=jnp.int32)
    route_hot = (route_all[:, None] == expert_range[None, :]).astype(jnp.int32)
    slot_rank = jnp.sum(jnp.cumsum(route_hot, axis=0) * route_hot, axis=-1) - 1
    target = (route_all * capacity + slot_rank).reshape(1, tiles, TILE, 1)
    places = jnp.arange(experts * capacity, dtype=jnp.int32).reshape(experts, 1, 1, capacity)
    onehot = (target == places).astype(BF16)
    chunks = 2 if capacity >= TILE else 1
    slots = capacity // chunks
    spread = max(1, TILE // capacity)
    merged = max(1, TILE // (slots * spread))

    def exchange(values):
        return lax.all_to_all(values, ("dp", "seq"), split_axis=0, concat_axis=0, tiled=True)

    def joined(values):
        if spread == 1:
            return values
        shape = values.shape
        values = values.reshape((-1, spread) + shape[1:])
        return jnp.moveaxis(values, 1, -2).reshape(
            (shape[0] // spread,) + shape[1:-1] + (spread * shape[-1],)
        )

    def parted(values):
        if spread == 1:
            return values
        shape = values.shape
        values = values.reshape(shape[:-1] + (spread, shape[-1] // spread))
        return jnp.moveaxis(values, -2, 1).reshape((-1,) + shape[1:-1] + (shape[-1] // spread,))

    half = tensor_count // 2
    grad_rows, row_pieces = lax.optimization_barrier((out_grad.astype(BF16), row_pieces))
    grad_shares = jnp.transpose(grad_rows.reshape(local_count, tensor_count, share), (1, 0, 2))
    grad_sent = jnp.stack(
        [grad_shares[jnp.array([j ^ (2 * k) for j in range(tensor_count)])] for k in range(half)],
        axis=1,
    )
    grad_here = lax.all_to_all(grad_sent, "tensor", split_axis=0, concat_axis=0, tiled=True)
    grad_here = jnp.moveaxis(grad_here, 1, 0).reshape(half, tiles, TILE, share)
    grad_buffer = einsum("knqd,enqs->ekds", grad_here, onehot).astype(BF16)

    queries = (einsum("nrd,dc->ncr", own_normed, in_full[:, 0]) * SCALE).astype(BF16)
    queries, grad_buffer = lax.optimization_barrier((queries, grad_buffer))
    keys_values = einsum("nrd,dkc->nkcr", normed_tiles, in_full[:, 1:]).astype(BF16)
    keys_values = keys_values.reshape(key_tiles, 2 * head_cols, TILE)
    grad_arrived = joined(exchange(grad_buffer))
    exact, attended, logs = attend(meta, queries, keys_values, bias)

    out_blocks = jnp.stack(relative(out_full))
    input_share = jnp.concatenate(
        [
            lax.dynamic_slice(
                own_tiles,
                (n ^ tensor_place if fast else n, 0, tensor_place * share),
                (1, TILE, share),
            )
            for n in range(tiles)
        ]
    )
    input_share = jnp.transpose(input_share, (0, 2, 1)).astype(F32)
    attn_kept = einsum("kec,ncq->kneq", out_blocks[0::2], attended)
    attn_sent = einsum("kec,ncq->kneq", out_blocks[1::2], attended)
    attn_share = sum_relative(attn_kept, attn_sent, "tensor")
    state_share = (input_share + attn_share).astype(BF16)
    grad_other = swap(grad_arrived, "tensor", 1)

    own = jnp.stack([grid_place, tensor_place]).astype(jnp.int32)
    router_t = jnp.transpose(router_weight)
    in_t, out_t = jnp.transpose(expert_in[0]), jnp.transpose(expert_out[0])
    weights = (
        expert_in[0],
        in_t,
        expert_out[0],
        router_weight,
        router_t,
        norm_gains[1][:, None],
    )
    arrivals = []
    for c in range(chunks):
        buffer = einsum("ndq,enqs->eds", state_share, onehot[..., c * slots : (c + 1) * slots])
        arrivals.append(joined(exchange(buffer.astype(BF16))))
    saved, parts_back = [], []
    small = jnp.zeros((experts + 1, width), F32)
    for c in range(chunks):
        kept, sent, normed_two, full, activated, pre_grad, gate, gain_sum, router_sum = run_expert(
            own,
            gather_relative(arrivals[c], "tensor"),
            (grad_arrived, grad_other),
            c,
            merged,
            weights,
        )
        saved.append((normed_two, full, activated, pre_grad, gate))
        parts_back.append((kept, sent))
        gain_part = jnp.sum(gain_sum, axis=1) / norm_gains[1]
        small = small + jnp.concatenate([router_sum, gain_part[None]])
    state_grad = jnp.transpose(grad_here[0], (0, 2, 1)).astype(F32)
    for c in range(chunks):
        total = parted(sum_relative(*parts_back[c], "tensor").astype(BF16))
        state_grad = state_grad + einsum(
            "eds,enqs->ndq", exchange(total), onehot[..., c * slots : (c + 1) * slots]
        )
    state_grad = state_grad.astype(BF16)
    result_kept, result_sent, grad_expert_in, grad_expert_out = run_result(
        own, saved, merged, out_t
    )
    result_total = sum_relative(result_kept, result_sent, "tensor").astype(BF16)
    state_grad, result_total = lax.optimization_barrier((state_grad, result_total))
    result_back = exchange(parted(result_total))

    branch = gather_relative(state_grad, "tensor")
    branch_tiles = jnp.stack(branch)
    attended_grad = einsum("kec,kneq->ncq", out_blocks, branch_tiles).astype(BF16)
    dq, dkv, bias_grad = attend_back(
        meta, queries, keys_values, bias, attended_grad, exact, logs
    )
    dq, dkv, bias_grad, result_back = lax.optimization_barrier((dq, dkv, bias_grad, result_back))

    own_slots = dkv[:tiles] if fast else lax.dynamic_slice_in_dim(dkv, seq_place * tiles, tiles, 0)
    in_flat = in_full.reshape(width, 3 * head_cols)
    own_part = einsum("ncq,dc->nqd", jnp.concatenate([dq, own_slots], axis=1), in_flat)
    in_grad = jnp.concatenate(
        [
            einsum("nqd,ncq->dc", own_normed, dq),
            einsum("nqd,ncq->dc", normed_tiles, dkv),
        ],
        axis=1,
    )
    if fast:
        far_part = einsum("ncq,dc->nqd", dkv[tiles:], in_flat[:, head_cols:])
        far_sum = sum_relative(far_part[0::2], far_part[1::2], "tensor")
        normed_one_grad = sum_relative(own_part[0::2], own_part[1::2], "tensor")
        normed_one_grad = normed_one_grad + swap(far_sum.astype(BF16), "seq", 1).astype(F32)
    else:
        all_part = einsum("ncq,dc->nqd", dkv, in_flat[:, head_cols:])
        own_part = einsum("ncq,dc->nqd", dq, in_flat[:, :head_cols])
        own_part = own_part + lax.psum_scatter(
            all_part.astype(BF16), "seq", scatter_dimension=0, tiled=True
        ).astype(F32)
        blocks = relative(own_part.reshape(group_count, width))
        normed_one_grad = sum_relative(jnp.stack(blocks[0::2]), jnp.stack(blocks[1::2]), "tensor")
    grad_attn_in = scatter_grid(in_grad.reshape(-1, attn_in_weight.shape[1], 3, head_cols))
    grad_attn_in = jnp.transpose(grad_attn_in, (1, 0, 2))
    gain_one_part = jnp.sum(in_grad * in_flat.astype(F32), axis=1) / norm_gains[0]
    own_branch = jnp.concatenate(
        reorder(
            [
                piece.reshape(tiles, share, TILE)[0]
                if tiles == 1
                else lax.dynamic_index_in_dim(piece, tensor_place, 0, keepdims=False)
                for piece in branch
            ],
            tensor_place,
        )
    )
    if local_count != TILE:
        own_branch = lax.dynamic_slice_in_dim(
            own_branch, tensor_place * local_count % TILE, local_count, 1
        )
    input_grad = jnp.transpose(own_branch).astype(F32) + norm_back(
        block_input, norm_gains[0], normed_one_grad
    )

    result_share = attn_share + einsum("eds,enqs->ndq", result_back, onehot)
    result_share = jnp.transpose(result_share.astype(BF16), (0, 2, 1)).reshape(group_count, share)
    result_rows = lax.all_to_all(
        result_share, "tensor", split_axis=0, concat_axis=1, tiled=True
    )
    block_out = block_input + result_rows.astype(F32)
    out_grads = einsum("ncq,kneq->kec", attended, branch_tiles)
    out_grads = jnp.concatenate(
        reorder([out_grads[k] for k in range(tensor_count)], tensor_place)
    )
    grad_attn_out = jnp.transpose(
        scatter_grid(out_grads.reshape(-1, attn_out_weight.shape[1], head_cols))
    )

    bias_padded = lax.dynamic_update_slice_in_dim(
        jnp.zeros((bucket_count, heads * tensor_count), F32),
        bias_sums(bias_grad, bucket_count),
        tensor_place * heads,
        1,
    )
    small = sum_all(
        jnp.concatenate([small.reshape(-1), gain_one_part, bias_padded.reshape(-1)]),
        ("tensor", "seq", "dp"),
    )
    first, second = experts * width, (experts + 1) * width
    grad_router = jnp.transpose(small[:first].reshape(experts, width))
    grad_gains = jnp.stack([small[second : second + width], small[first:second]])
    bias_sum = small[second + width :].reshape(bucket_count, heads * tensor_count)
    grad_bias = lax.dynamic_slice_in_dim(bias_sum, tensor_place * heads, heads, 1)
    return (
        block_out,
        input_grad,
        grad_attn_in,
        grad_attn_out,
        grad_bias,
        grad_gains,
        grad_router,
        grad_expert_in[None],
        grad_expert_out[None],
    )


def solution(mesh):
    return jax.shard_map(
        shards,
        mesh=mesh,
        in_specs=(
            P(("dp", "seq", "tensor"), None),
            P(None, ("dp", "seq"), "tensor"),
            P("tensor", ("dp", "seq")),
            P(None, "tensor"),
            P(),
            P(),
            P(("dp", "seq"), None, "tensor"),
            P(("dp", "seq"), "tensor", None),
            P("dp", ("seq", "tensor")),
            P(("dp", "seq"), None),
            P(("dp", "seq", "tensor"), None),
        ),
        out_specs=(
            P(("dp", "seq", "tensor"), None),
            P(("dp", "seq", "tensor"), None),
            P(None, ("dp", "seq"), "tensor"),
            P("tensor", ("dp", "seq")),
            P(None, "tensor"),
            P(),
            P(),
            P(("dp", "seq"), None, "tensor"),
            P(("dp", "seq"), "tensor", None),
        ),
        check_vma=False,
    )
```

profile of v0, /device:TPU:0, one launch (start us, length us, event | category | flops | bytes accessed | tf_op | source)
XLA Modules:
  0.0 482.3 jit_solution(12381659442267320731)
XLA Ops:
  3.2 3.0 collective-permute-start.8
  7.8 2.5 collective-permute-start.6
  16.1 2.3 reduce-window.6
  23.3 2.6 select_add_fusion
  41.0 6.2 %collective-permute-done.7 = bf16[3,96,4,192]{3,1,2,0:T(8,128)(2,1)S(1)} collective-permute-done((bf16[3,96,4,192]{3,1,2,0:T(8,128)(2,1)S(1)}, bf16[3,96,4,192]{3,1,2,0:T(8,128)(2,1)S(1)}, u32[]{:S(2)}, u32[]{:S(2)}) %collective-permute-start.7) | collective-permute-done | bytes 442400 | tf_op jit(solution)/shard_map/ppermute | solution.py:42
  55.0 4.5 collective-permute-done.2
  60.3 2.8 copy.346
  63.1 3.8 reshape.907
  83.5 4.4 all-to-all-start
  102.4 4.5 fusion.33
  107.0 4.3 all-to-all-start.2
  111.3 25.0 %attend.1 = (f32[4,192,256]{2,1,0:T(8,128)S(1)}, bf16[4,192,256]{2,1,0:T(8,128)(2,1)S(1)}, f32[4,3,1,256]{3,2,1,0:T(1,128)S(1)}) custom-call(s32[15]{0:T(128)S(1)} %concatenate.72.meta_ref, bf16[4,192,256]{2,1,0:T(8,128)(2,1)S(1)} %fusion.97.q_ref, bf16[8,384,256]{2,1,0:T(8,128)(2,1)S(1)} %bitcast.529, f32[5,3,256,256]{3,2,1,0:T(8,128)} %broadcast_multiply_fusion.bias_ref), custom_call_target="tpu_custom_call" | custom-call | flops 1610612736 | bytes 16777216 | tf_op jit(solution)/shard_map/attend/pallas_call | solution.py:276
  146.8 3.1 broadcast_compare_fusion
  150.4 9.1 %collective-permute-done.10 = bf16[1,4,192,256]{2,3,1,0:T(8,128)(2,1)} collective-permute-done((bf16[1,4,192,256]{2,3,1,0:T(8,128)(2,1)}, bf16[1,4,192,256]{2,3,1,0:T(8,128)(2,1)}, u32[]{:S(2)}, u32[]{:S(2)}) %collective-permute-start.10) | collective-permute-done | bytes 393248 | tf_op jit(solution)/shard_map/ppermute | solution.py:42
  163.1 3.5 all-to-all-start.1
  166.6 3.0 fusion.94
  169.6 8.5 %all-to-all-done.1.refs_0_ = bf16[8,192,128]{2,1,0:T(8,128)(2,1)S(1)} async-done(((bf16[8,192,128]{2,1,0:T(8,128)(2,1)}), bf16[8,192,128]{2,1,0:T(8,128)(2,1)S(1)}, u32[]{:S(2)}, u32[]{:S(2)}) %all-to-all-start.1) | async-done | bytes 393248 | tf_op jit(solution)/shard_map/all_to_all | solution.py:721
  178.9 3.8 all-to-all-start.4
  184.2 10.0 %all-to-all-done.4.refs_0_ = bf16[8,192,128]{2,1,0:T(8,128)(2,1)S(1)} async-done(((bf16[8,192,128]{2,1,0:T(8,128)(2,1)}), bf16[8,192,128]{2,1,0:T(8,128)(2,1)S(1)}, u32[]{:S(2)}, u32[]{:S(2)}) %all-to-all-start.4) | async-done | bytes 393248 | tf_op jit(solution)/shard_map/all_to_all | solution.py:721
  195.8 6.3 %collective-permute-done.18.refs_2_ = bf16[8,192,128]{2,1,0:T(8,128)(2,1)} collective-permute-done((bf16[8,192,128]{2,1,0:T(8,128)(2,1)S(1)}, bf16[8,192,128]{2,1,0:T(8,128)(2,1)}, u32[]{:S(2)}, u32[]{:S(2)}) %collective-permute-start.18) | collective-permute-done | bytes 393248 | tf_op jit(solution)/shard_map/ppermute | solution.py:42
  206.7 2.4 copy.360
  212.6 16.6 %expert.2 = (bf16[2,8,192,128]{3,2,1,0:T(8,128)(2,1)S(1)}, bf16[2,8,192,128]{3,2,1,0:T(8,128)(2,1)S(1)}, bf16[4,768,256]{2,1,0:T(8,128)(2,1)}, bf16[4,4,192,256]...) custom-call(s32[2]{0:T(128)S(1)} %copy-done.14, ...), custom_call_target="tpu_custom_call" | custom-call | flops 3623878656 | bytes 12582912 | tf_op jit(solution)/shard_map/expert/pallas_call | solution.py:530
  231.2 16.9 %expert.3 = (bf16[2,8,192,128]{3,2,1,0:T(8,128)(2,1)S(1)}, bf16[2,8,192,128]{3,2,1,0:T(8,128)(2,1)S(1)}, bf16[4,768,256]{2,1,0:T(8,128)(2,1)}, bf16[4,4,192,256]...) custom-call(s32[2]{0:T(128)S(1)} %copy-done.15, ...), custom_call_target="tpu_custom_call" | custom-call | flops 3623878656 | bytes 12582912 | tf_op jit(solution)/shard_map/expert/pallas_call | solution.py:530
  249.1 13.7 %result.1 = (bf16[2,8,192,256]{3,2,1,0:T(8,128)(2,1)S(1)}, bf16[2,8,192,256]{3,2,1,0:T(8,128)(2,1)}, f32[768,768]{1,0:T(8,128)}, f32[768,768]{1,0:T(8,128)}) custom-call(s32[2]{0:T(128)S(1)} %copy-done.15, bf16[4,768,256]{2,1,0:T(8,128)(2,1)S(1)} %copy-done.18, bf16[4,4,192,256]{3,2,1,0:T(8,128)(2,1)} %get-tuple-element.55.refs_1_, ...), custom_call_target="tpu_custom_call" | custom-call | flops 7247757312 | bytes 18874368 | tf_op jit(solution)/shard_map/result/pallas_call | solution.py:586
  267.8 7.8 %collective-permute-done.16 = bf16[1,8,192,128]{3,2,1,0:T(8,128)(2,1)S(1)} collective-permute-done((bf16[1,8,192,128]{3,2,1,0:T(8,128)(2,1)S(1)}, bf16[1,8,192,128]{3,2,1,0:T(8,128)(2,1)S(1)}, u32[]{:S(2)}, u32[]{:S(2)}) %collective-permute-start.16) | collective-permute-done | bytes 393248 | tf_op jit(solution)/shard_map/ppermute | solution.py:42
  276.4 6.1 %all-to-all-start.3 = ((bf16[8,192,128]{2,1,0:T(8,128)(2,1)}), bf16[8,192,128]{2,1,0:T(8,128)(2,1)}, u32[]{:S(2)}, u32[]{:S(2)}) async-start(bf16[8,192,128]{2,1,0:T(8,128)(2,1)} %fusion.143), calls=%async_computation.3 | async-start | bytes 786432 | tf_op jit(solution)/shard_map/all_to_all | solution.py:721
  285.3 3.5 add_bitcast_fusion
  288.8 4.0 all-to-all-done.3
  292.7 4.5 all-to-all-start.5
  301.2 3.1 fusion.68
  304.3 3.4 all-to-all-done.5
  307.7 3.4 fusion.100
  311.1 5.7 %collective-permute-done.23 = bf16[1,8,192,256]{3,2,1,0:T(8,128)(2,1)} collective-permute-done((bf16[1,8,192,256]{3,2,1,0:T(8,128)(2,1)S(1)}, bf16[1,8,192,256]{3,2,1,0:T(8,128)(2,1)}, u32[]{:S(2)}, u32[]{:S(2)}) %collective-permute-start.23) | collective-permute-done | bytes 786464 | tf_op jit(solution)/shard_map/ppermute | solution.py:42
  316.8 2.3 fusion.123
  320.2 7.6 %collective-permute-done.25 = bf16[4,192,256]{2,1,0:T(8,128)(2,1)} collective-permute-done((bf16[4,192,256]{2,1,0:T(8,128)(2,1)}, bf16[4,192,256]{2,1,0:T(8,128)(2,1)}, u32[]{:S(2)}, u32[]{:S(2)}) %collective-permute-start.25) | collective-permute-done | bytes 393248 | tf_op jit(solution)/shard_map/ppermute | solution.py:42
  333.6 5.5 %all-to-all-start.6 = ((bf16[8,192,256]{2,1,0:T(8,128)(2,1)}), bf16[8,192,256]{2,1,0:T(8,128)(2,1)}, u32[]{:S(2)}, u32[]{:S(2)}) async-start(bf16[8,192,256]{2,1,0:T(8,128)(2,1)} %fusion.123), calls=%async_computation.6 | async-start | bytes 1572864 | tf_op jit(solution)/shard_map/all_to_all | solution.py:721
  345.4 29.0 %attend_back.1 = (bf16[4,192,256]{2,1,0:T(8,128)(2,1)S(1)}, bf16[8,384,256]{2,1,0:T(8,128)(2,1)S(1)}, f32[5,3,256,256]{3,2,1,0:T(8,128)}) custom-call(s32[15]{0:T(128)S(1)} %concatenate.72.meta_ref, bf16[4,192,256]{2,1,0:T(8,128)(2,1)S(1)} %copy-done.17, bf16[8,384,256]{2,1,0:T(8,128)(2,1)S(1)} %bitcast.530, ...), custom_call_target="tpu_custom_call" | custom-call | flops 4026531840 | bytes 16777216 | tf_op jit(solution)/shard_map/attend_back/pallas_call | solution.py:370
  374.7 4.3 collective-permute-start.37
  382.1 3.4 convolution_bitcast_fusion
  396.2 2.8 fusion.221
  399.9 3.1 fusion.222
  407.8 2.8 fusion.87
  416.0 3.5 all-to-all-start.7
  450.9 8.0 %collective-permute-done.30 = bf16[1,256,768]{1,2,0:T(8,128)(2,1)S(1)} collective-permute-done((bf16[1,256,768]{1,2,0:T(8,128)(2,1)S(1)}, bf16[1,256,768]{1,2,0:T(8,128)(2,1)S(1)}, u32[]{:S(2)}, u32[]{:S(2)}) %collective-permute-start.30) | collective-permute-done | bytes 393248 | tf_op jit(solution)/shard_map/ppermute | solution.py:42
  465.5 3.3 collective-permute-done.35
  468.8 4.7 collective-permute-done.34
  476.1 2.5 bitcast_add_fusion.3
  478.7 2.3 copy.390
  (616 shorter events, 189.8 us)
Async XLA Ops:
  3.2 37.7 %collective-permute-start.8 = (bf16[96,4,192]{2,0,1:T(8,128)(2,1)}, bf16[96,4,192]{2,0,1:T(8,128)(2,1)}, u32[]{:S(2)}, u32[]{:S(2)}) collective-permute-start(bf16[96,4,192]{2,0,1:T(8,128)(2,1)} %pad_maximum_fusion.17), channel_id=1, source_target_pairs={{0,4},{4,0},{1,5},{5,1},{2,6},{6,2},{3,7},{7,3},{8,12},{12,8},{9,1... | collective-permute-start | bytes 442376 | tf_op jit(solution)/shard_map/ppermute | solution.py:42
  6.2 25.6 %collective-permute-start.4 = (bf16[96,4,192]{2,0,1:T(8,128)(2,1)}, bf16[96,4,192]{2,0,1:T(8,128)(2,1)}, u32[]{:S(2)}, u32[]{:S(2)}) collective-permute-start(bf16[96,4,192]{2,0,1:T(8,128)(2,1)} %pad_maximum_fusion.17), channel_id=1, source_target_pairs={{0,8},{8,0},{16,24},{24,16},{1,9},{9,1},{17,25},{25,17},{2,10},{10... | collective-permute-start | bytes 442376 | tf_op jit(solution)/shard_map/ppermute | solution.py:42
  7.8 24.0 %collective-permute-start.6 = (bf16[96,4,192]{2,0,1:T(8,128)(2,1)}, bf16[96,4,192]{2,0,1:T(8,128)(2,1)}, u32[]{:S(2)}, u32[]{:S(2)}) collective-permute-start(bf16[96,4,192]{2,0,1:T(8,128)(2,1)} %pad_maximum_fusion.17), channel_id=1, source_target_pairs={{0,24},{8,16},{16,8},{24,0},{1,25},{9,17},{17,9},{25,1},{2,26},{10... | collective-permute-start | bytes 442376 | tf_op jit(solution)/shard_map/ppermute | solution.py:42
  10.2 21.6 %collective-permute-start.5 = (bf16[96,4,192]{2,0,1:T(8,128)(2,1)}, bf16[96,4,192]{2,0,1:T(8,128)(2,1)}, u32[]{:S(2)}, u32[]{:S(2)}) collective-permute-start(bf16[96,4,192]{2,0,1:T(8,128)(2,1)} %pad_maximum_fusion.17), channel_id=1, source_target_pairs={{0,16},{8,24},{16,0},{24,8},{1,17},{9,25},{17,1},{25,9},{2,18},{10... | collective-permute-start | bytes 442376 | tf_op jit(solution)/shard_map/ppermute | solution.py:42
  14.1 22.0 %collective-permute-start = (bf16[272,768]{1,0:T(8,128)(2,1)}, bf16[272,768]{1,0:T(8,128)(2,1)}, u32[]{:S(2)}, u32[]{:S(2)}) collective-permute-start(bf16[272,768]{1,0:T(8,128)(2,1)} %get-tuple-element.307), channel_id=1, source_target_pairs={{0,4},{4,0},{1,5},{5,1},{2,6},{6,2},{3,7},{7,3},{8,12},{12,8},{9,1... | collective-permute-start | bytes 1253384 | tf_op jit(solution)/shard_map/ppermute | solution.py:42
  33.1 14.0 %collective-permute-start.7 = (bf16[3,96,4,192]{3,1,2,0:T(8,128)(2,1)S(1)}, bf16[3,96,4,192]{3,1,2,0:T(8,128)(2,1)S(1)}, u32[]{:S(2)}, u32[]{:S(2)}) collective-permute-start(bf16[3,96,4,192]{3,1,2,0:T(8,128)(2,1)S(1)} %pad_maximum_fusion.11), channel_id=1, source_target_pairs={{0,4},{4,0},{1,5},{5,1},{2,6},{6,2},{3,7},{7,3},{8,12},{12,8},{9,1... | collective-permute-start | bytes 1327112 | tf_op jit(solution)/shard_map/ppermute | solution.py:42
  38.2 35.5 %collective-permute-start.1 = (bf16[2,272,768]{2,1,0:T(8,128)(2,1)}, bf16[2,272,768]{2,1,0:T(8,128)(2,1)}, u32[]{:S(2)}, u32[]{:S(2)}) collective-permute-start(bf16[2,272,768]{2,1,0:T(8,128)(2,1)} %pad_maximum_fusion.7), channel_id=1, source_target_pairs={{0,1},{1,0},{2,3},{3,2},{4,5},{5,4},{6,7},{7,6},{8,9},{9,8},{10,11... | collective-permute-start | bytes 2506760 | tf_op jit(solution)/shard_map/ppermute | solution.py:42
  38.2 21.3 %collective-permute-start.2 = (bf16[2,272,768]{2,1,0:T(8,128)(2,1)}, bf16[2,272,768]{2,1,0:T(8,128)(2,1)}, u32[]{:S(2)}, u32[]{:S(2)}) collective-permute-start(bf16[2,272,768]{2,1,0:T(8,128)(2,1)} %pad_maximum_fusion.7), channel_id=1, source_target_pairs={{0,2},{1,3},{2,0},{3,1},{4,6},{5,7},{6,4},{7,5},{8,10},{9,11},{10,... | collective-permute-start | bytes 2506760 | tf_op jit(solution)/shard_map/ppermute | solution.py:42
  59.5 19.1 %collective-permute-start.3 = (bf16[2,272,768]{2,1,0:T(8,128)(2,1)}, bf16[2,272,768]{2,1,0:T(8,128)(2,1)}, u32[]{:S(2)}, u32[]{:S(2)}) collective-permute-start(bf16[2,272,768]{2,1,0:T(8,128)(2,1)} %collective-permute-done.2), channel_id=1, source_target_pairs={{0,1},{1,0},{2,3},{3,2},{4,5},{5,4},{6,7},{7,6},{8,9},{9,8},{10,11... | collective-permute-start | bytes 2506760 | tf_op jit(solution)/shard_map/ppermute | solution.py:42
  83.5 18.9 %all-to-all-start = ((bf16[4,2,256,192]{2,3,1,0:T(8,128)(2,1)}), bf16[4,2,256,192]{2,3,1,0:T(8,128)(2,1)}, u32[]{:S(2)}, u32[]{:S(2)}) async-start(bf16[4,2,256,192]{2,3,1,0:T(8,128)(2,1)} %copy.348), calls=%async_computation | async-start | bytes 1572864 | tf_op jit(solution)/shard_map/all_to_all | solution.py:746
  107.0 56.1 %all-to-all-start.2 = ((bf16[8,2,192,256]{3,2,1,0:T(8,128)(2,1)}), bf16[8,2,192,256]{3,2,1,0:T(8,128)(2,1)}, u32[]{:S(2)}, u32[]{:S(2)}) async-start(bf16[8,2,192,256]{3,2,1,0:T(8,128)(2,1)} %fusion.33), calls=%async_computation.2 | async-start | bytes 3145728 | tf_op jit(solution)/shard_map/all_to_all | solution.py:721
  144.9 14.5 %collective-permute-start.10 = (bf16[1,4,192,256]{2,3,1,0:T(8,128)(2,1)}, bf16[1,4,192,256]{2,3,1,0:T(8,128)(2,1)}, u32[]{:S(2)}, u32[]{:S(2)}) collective-permute-start(bf16[1,4,192,256]{2,3,1,0:T(8,128)(2,1)} %fusion.141), channel_id=1, source_target_pairs={{0,2},{1,3},{2,0},{3,1},{4,6},{5,7},{6,4},{7,5},{8,10},{9,11},{10,... | collective-permute-start | bytes 1179656 | tf_op jit(solution)/shard_map/ppermute | solution.py:42
  163.1 15.1 %all-to-all-start.1 = ((bf16[8,192,128]{2,1,0:T(8,128)(2,1)}), bf16[8,192,128]{2,1,0:T(8,128)(2,1)S(1)}, u32[]{:S(2)}, u32[]{:S(2)}) async-start(bf16[8,192,128]{2,1,0:T(8,128)(2,1)} %fusion.91), calls=%async_computation.1 | async-start | bytes 786432 | tf_op jit(solution)/shard_map/all_to_all | solution.py:721
  166.5 42.5 %collective-permute-start.14 = (bf16[8,2,192,256]{3,2,1,0:T(8,128)(2,1)}, bf16[8,2,192,256]{3,2,1,0:T(8,128)(2,1)}, u32[]{:S(2)}, u32[]{:S(2)}) collective-permute-start(bf16[8,2,192,256]{3,2,1,0:T(8,128)(2,1)} %all-to-all-done.2.refs_4_), channel_id=1, source_target_pairs={{0,1},{1,0},{2,3},{3,2},{4,5},{5,4},{6,7},{7,6},{8,9},{9,8},{10,11... | collective-permute-start | bytes 4718600 | tf_op jit(solution)/shard_map/ppermute | solution.py:42
  178.9 15.4 %all-to-all-start.4 = ((bf16[8,192,128]{2,1,0:T(8,128)(2,1)}), bf16[8,192,128]{2,1,0:T(8,128)(2,1)S(1)}, u32[]{:S(2)}, u32[]{:S(2)}) async-start(bf16[8,192,128]{2,1,0:T(8,128)(2,1)} %fusion.94), calls=%async_computation.4 | async-start | bytes 786432 | tf_op jit(solution)/shard_map/all_to_all | solution.py:721
  182.7 12.6 %collective-permute-start.12 = (bf16[8,192,128]{2,1,0:T(8,128)(2,1)}, bf16[8,192,128]{2,1,0:T(8,128)(2,1)}, u32[]{:S(2)}, u32[]{:S(2)}) collective-permute-start(bf16[8,192,128]{2,1,0:T(8,128)(2,1)} %copy-done.6), channel_id=1, source_target_pairs={{0,2},{1,3},{2,0},{3,1},{4,6},{5,7},{6,4},{7,5},{8,10},{9,11},{10,... | collective-permute-start | bytes 1179656 | tf_op jit(solution)/shard_map/ppermute | solution.py:42
  194.3 7.9 %collective-permute-start.18 = (bf16[8,192,128]{2,1,0:T(8,128)(2,1)S(1)}, bf16[8,192,128]{2,1,0:T(8,128)(2,1)}, u32[]{:S(2)}, u32[]{:S(2)}) collective-permute-start(bf16[8,192,128]{2,1,0:T(8,128)(2,1)S(1)} %all-to-all-done.4.refs_0_), channel_id=1, source_target_pairs={{0,2},{1,3},{2,0},{3,1},{4,6},{5,7},{6,4},{7,5},{8,10},{9,11},{10,... | collective-permute-start | bytes 1179656 | tf_op jit(solution)/shard_map/ppermute | solution.py:42
  195.3 13.7 %collective-permute-start.11 = (bf16[8,192,128]{2,1,0:T(8,128)(2,1)}, bf16[8,192,128]{2,1,0:T(8,128)(2,1)}, u32[]{:S(2)}, u32[]{:S(2)}) collective-permute-start(bf16[8,192,128]{2,1,0:T(8,128)(2,1)} %copy-done.6), channel_id=1, source_target_pairs={{0,1},{1,0},{2,3},{3,2},{4,5},{5,4},{6,7},{7,6},{8,9},{9,8},{10,11... | collective-permute-start | bytes 1179656 | tf_op jit(solution)/shard_map/ppermute | solution.py:42
  195.3 13.7 %collective-permute-start.13 = (bf16[8,192,128]{2,1,0:T(8,128)(2,1)}, bf16[8,192,128]{2,1,0:T(8,128)(2,1)}, u32[]{:S(2)}, u32[]{:S(2)}) collective-permute-start(bf16[8,192,128]{2,1,0:T(8,128)(2,1)} %collective-permute-done.12.refs_2_), channel_id=1, source_target_pairs={{0,1},{1,0},{2,3},{3,2},{4,5},{5,4},{6,7},{7,6},{8,9},{9,8},{10,11... | collective-permute-start | bytes 1179656 | tf_op jit(solution)/shard_map/ppermute | solution.py:42
  195.8 35.4 %collective-permute-start.17 = (bf16[8,192,128]{2,1,0:T(8,128)(2,1)S(1)}, bf16[8,192,128]{2,1,0:T(8,128)(2,1)}, u32[]{:S(2)}, u32[]{:S(2)}) collective-permute-start(bf16[8,192,128]{2,1,0:T(8,128)(2,1)S(1)} %all-to-all-done.4.refs_0_), channel_id=1, source_target_pairs={{0,1},{1,0},{2,3},{3,2},{4,5},{5,4},{6,7},{7,6},{8,9},{9,8},{10,11... | collective-permute-start | bytes 1179656 | tf_op jit(solution)/shard_map/ppermute | solution.py:42
  202.2 29.0 %collective-permute-start.19 = (bf16[8,192,128]{2,1,0:T(8,128)(2,1)}, bf16[8,192,128]{2,1,0:T(8,128)(2,1)}, u32[]{:S(2)}, u32[]{:S(2)}) collective-permute-start(bf16[8,192,128]{2,1,0:T(8,128)(2,1)} %collective-permute-done.18.refs_2_), channel_id=1, source_target_pairs={{0,1},{1,0},{2,3},{3,2},{4,5},{5,4},{6,7},{7,6},{8,9},{9,8},{10,11... | collective-permute-start | bytes 1179656 | tf_op jit(solution)/shard_map/ppermute | solution.py:42
  230.7 32.6 %collective-permute-start.15 = (bf16[2,8,192,128]{3,2,1,0:T(8,128)(2,1)S(1)}, bf16[2,8,192,128]{3,2,1,0:T(8,128)(2,1)S(1)}, u32[]{:S(2)}, u32[]{:S(2)}) collective-permute-start(bf16[2,8,192,128]{3,2,1,0:T(8,128)(2,1)S(1)} %get-tuple-element.51), channel_id=1, source_target_pairs={{0,1},{1,0},{2,3},{3,2},{4,5},{5,4},{6,7},{7,6},{8,9},{9,8},{10,11... | collective-permute-start | bytes 2359304 | tf_op jit(solution)/shard_map/ppermute | solution.py:42
  249.1 15.8 %collective-permute-start.20 = (bf16[2,8,192,128]{3,2,1,0:T(8,128)(2,1)S(1)}, bf16[2,8,192,128]{3,2,1,0:T(8,128)(2,1)S(1)}, u32[]{:S(2)}, u32[]{:S(2)}) collective-permute-start(bf16[2,8,192,128]{3,2,1,0:T(8,128)(2,1)S(1)} %get-tuple-element.53), channel_id=1, source_target_pairs={{0,1},{1,0},{2,3},{3,2},{4,5},{5,4},{6,7},{7,6},{8,9},{9,8},{10,11... | collective-permute-start | bytes 2359304 | tf_op jit(solution)/shard_map/ppermute | solution.py:42
  262.7 22.6 %collective-permute-start.22 = (bf16[2,8,192,256]{3,2,1,0:T(8,128)(2,1)}, bf16[2,8,192,256]{3,2,1,0:T(8,128)(2,1)}, u32[]{:S(2)}, u32[]{:S(2)}) collective-permute-start(bf16[2,8,192,256]{3,2,1,0:T(8,128)(2,1)} %get-tuple-element.65), channel_id=1, source_target_pairs={{0,1},{1,0},{2,3},{3,2},{4,5},{5,4},{6,7},{7,6},{8,9},{9,8},{10,11... | collective-permute-start | bytes 4718600 | tf_op jit(solution)/shard_map/ppermute | solution.py:42
  263.6 12.0 %collective-permute-start.16 = (bf16[1,8,192,128]{3,2,1,0:T(8,128)(2,1)S(1)}, bf16[1,8,192,128]{3,2,1,0:T(8,128)(2,1)S(1)}, u32[]{:S(2)}, u32[]{:S(2)}) collective-permute-start(bf16[1,8,192,128]{3,2,1,0:T(8,128)(2,1)S(1)} %fusion.144), channel_id=1, source_target_pairs={{0,2},{1,3},{2,0},{3,1},{4,6},{5,7},{6,4},{7,5},{8,10},{9,11},{10,... | collective-permute-start | bytes 1179656 | tf_op jit(solution)/shard_map/ppermute | solution.py:42
  267.0 16.2 %collective-permute-start.21 = (bf16[1,8,192,128]{3,2,1,0:T(8,128)(2,1)}, bf16[1,8,192,128]{3,2,1,0:T(8,128)(2,1)}, u32[]{:S(2)}, u32[]{:S(2)}) collective-permute-start(bf16[1,8,192,128]{3,2,1,0:T(8,128)(2,1)} %fusion.146), channel_id=1, source_target_pairs={{0,2},{1,3},{2,0},{3,1},{4,6},{5,7},{6,4},{7,5},{8,10},{9,11},{10,... | collective-permute-start | bytes 1179656 | tf_op jit(solution)/shard_map/ppermute | solution.py:42
  276.4 16.3 %all-to-all-start.3 = ((bf16[8,192,128]{2,1,0:T(8,128)(2,1)}), bf16[8,192,128]{2,1,0:T(8,128)(2,1)}, u32[]{:S(2)}, u32[]{:S(2)}) async-start(bf16[8,192,128]{2,1,0:T(8,128)(2,1)} %fusion.143), calls=%async_computation.3 | async-start | bytes 786432 | tf_op jit(solution)/shard_map/all_to_all | solution.py:721
  292.7 15.0 %all-to-all-start.5 = ((bf16[8,192,128]{2,1,0:T(8,128)(2,1)}), bf16[8,192,128]{2,1,0:T(8,128)(2,1)}, u32[]{:S(2)}, u32[]{:S(2)}) async-start(bf16[8,192,128]{2,1,0:T(8,128)(2,1)} %fusion.145), calls=%async_computation.5 | async-start | bytes 786432 | tf_op jit(solution)/shard_map/all_to_all | solution.py:721
  298.9 17.9 %collective-permute-start.23 = (bf16[1,8,192,256]{3,2,1,0:T(8,128)(2,1)S(1)}, bf16[1,8,192,256]{3,2,1,0:T(8,128)(2,1)}, u32[]{:S(2)}, u32[]{:S(2)}) collective-permute-start(bf16[1,8,192,256]{3,2,1,0:T(8,128)(2,1)S(1)} %fusion.124), channel_id=1, source_target_pairs={{0,2},{1,3},{2,0},{3,1},{4,6},{5,7},{6,4},{7,5},{8,10},{9,11},{10,... | collective-permute-start | bytes 2359304 | tf_op jit(solution)/shard_map/ppermute | solution.py:42
  319.1 8.7 %collective-permute-start.25 = (bf16[4,192,256]{2,1,0:T(8,128)(2,1)}, bf16[4,192,256]{2,1,0:T(8,128)(2,1)}, u32[]{:S(2)}, u32[]{:S(2)}) collective-permute-start(bf16[4,192,256]{2,1,0:T(8,128)(2,1)} %fusion.100), channel_id=1, source_target_pairs={{0,2},{1,3},{2,0},{3,1},{4,6},{5,7},{6,4},{7,5},{8,10},{9,11},{10,... | collective-permute-start | bytes 1179656 | tf_op jit(solution)/shard_map/ppermute | solution.py:42
  320.2 18.9 %collective-permute-start.24 = (bf16[4,192,256]{2,1,0:T(8,128)(2,1)}, bf16[4,192,256]{2,1,0:T(8,128)(2,1)}, u32[]{:S(2)}, u32[]{:S(2)}) collective-permute-start(bf16[4,192,256]{2,1,0:T(8,128)(2,1)} %fusion.100), channel_id=1, source_target_pairs={{0,1},{1,0},{2,3},{3,2},{4,5},{5,4},{6,7},{7,6},{8,9},{9,8},{10,11... | collective-permute-start | bytes 1179656 | tf_op jit(solution)/shard_map/ppermute | solution.py:42
  327.8 11.2 %collective-permute-start.26 = (bf16[4,192,256]{2,1,0:T(8,128)(2,1)}, bf16[4,192,256]{2,1,0:T(8,128)(2,1)}, u32[]{:S(2)}, u32[]{:S(2)}) collective-permute-start(bf16[4,192,256]{2,1,0:T(8,128)(2,1)} %collective-permute-done.25), channel_id=1, source_target_pairs={{0,1},{1,0},{2,3},{3,2},{4,5},{5,4},{6,7},{7,6},{8,9},{9,8},{10,11... | collective-permute-start | bytes 1179656 | tf_op jit(solution)/shard_map/ppermute | solution.py:42
  333.6 48.5 %all-to-all-start.6 = ((bf16[8,192,256]{2,1,0:T(8,128)(2,1)}), bf16[8,192,256]{2,1,0:T(8,128)(2,1)}, u32[]{:S(2)}, u32[]{:S(2)}) async-start(bf16[8,192,256]{2,1,0:T(8,128)(2,1)} %fusion.123), calls=%async_computation.6 | async-start | bytes 1572864 | tf_op jit(solution)/shard_map/all_to_all | solution.py:721
  341.3 33.1 %collective-permute-start.36 = (bf16[4,96,192]{2,1,0:T(8,128)(2,1)S(1)}, bf16[4,96,192]{2,1,0:T(8,128)(2,1)S(1)}, u32[]{:S(2)}, u32[]{:S(2)}) collective-permute-start(bf16[4,96,192]{2,1,0:T(8,128)(2,1)S(1)} %pad_maximum_fusion.18), channel_id=1, source_target_pairs={{0,4},{4,0},{1,5},{5,1},{2,6},{6,2},{3,7},{7,3},{8,12},{12,8},{9,1... | collective-permute-start | bytes 442376 | tf_op jit(solution)/shard_map/ppermute | solution.py:42
  374.5 6.3 %collective-permute-start.39 = (bf16[96,192]{1,0:T(8,128)(2,1)S(1)}, bf16[96,192]{1,0:T(8,128)(2,1)S(1)}, u32[]{:S(2)}, u32[]{:S(2)}) collective-permute-start(bf16[96,192]{1,0:T(8,128)(2,1)S(1)} %get-tuple-element.294), channel_id=1, source_target_pairs={{0,24},{8,16},{16,8},{24,0},{1,25},{9,17},{17,9},{25,1},{2,26},{10... | collective-permute-start | bytes 110600 | tf_op jit(solution)/shard_map/ppermute | solution.py:42
  374.6 6.2 %collective-permute-start.38 = (bf16[96,192]{1,0:T(8,128)(2,1)S(1)}, bf16[96,192]{1,0:T(8,128)(2,1)S(1)}, u32[]{:S(2)}, u32[]{:S(2)}) collective-permute-start(bf16[96,192]{1,0:T(8,128)(2,1)S(1)} %get-tuple-element.293), channel_id=1, source_target_pairs={{0,16},{8,24},{16,0},{24,8},{1,17},{9,25},{17,1},{25,9},{2,18},{10... | collective-permute-start | bytes 110600 | tf_op jit(solution)/shard_map/ppermute | solution.py:42
  374.7 6.6 %collective-permute-start.37 = (bf16[96,192]{1,0:T(8,128)(2,1)S(1)}, bf16[96,192]{1,0:T(8,128)(2,1)S(1)}, u32[]{:S(2)}, u32[]{:S(2)}) collective-permute-start(bf16[96,192]{1,0:T(8,128)(2,1)S(1)} %get-tuple-element.214), channel_id=1, source_target_pairs={{0,8},{8,0},{16,24},{24,16},{1,9},{9,1},{17,25},{25,17},{2,10},{10... | collective-permute-start | bytes 110600 | tf_op jit(solution)/shard_map/ppermute | solution.py:42
  399.9 45.5 %collective-permute-start.29 = (bf16[2,256,768]{1,2,0:T(8,128)(2,1)}, bf16[2,256,768]{1,2,0:T(8,128)(2,1)}, u32[]{:S(2)}, u32[]{:S(2)}) collective-permute-start(bf16[2,256,768]{1,2,0:T(8,128)(2,1)} %slice.539), channel_id=1, source_target_pairs={{0,1},{1,0},{2,3},{3,2},{4,5},{5,4},{6,7},{7,6},{8,9},{9,8},{10,11... | collective-permute-start | bytes 2359304 | tf_op jit(solution)/shard_map/ppermute | solution.py:42
  404.2 44.7 %collective-permute-start.27 = (bf16[2,256,768]{1,2,0:T(8,128)(2,1)}, bf16[2,256,768]{1,2,0:T(8,128)(2,1)}, u32[]{:S(2)}, u32[]{:S(2)}) collective-permute-start(bf16[2,256,768]{1,2,0:T(8,128)(2,1)} %slice.533), channel_id=1, source_target_pairs={{0,1},{1,0},{2,3},{3,2},{4,5},{5,4},{6,7},{7,6},{8,9},{9,8},{10,11... | collective-permute-start | bytes 2359304 | tf_op jit(solution)/shard_map/ppermute | solution.py:42
  416.0 59.5 %all-to-all-start.7 = ((bf16[4,256,192]{1,2,0:T(8,128)(2,1)}), bf16[4,256,192]{1,2,0:T(8,128)(2,1)S(1)}, u32[]{:S(2)}, u32[]{:S(2)}) async-start(bf16[4,256,192]{1,2,0:T(8,128)(2,1)} %copy.372), calls=%async_computation.7 | async-start | bytes 786432 | tf_op jit(solution)/shard_map/all_to_all | solution.py:874
  425.2 12.6 %collective-permute-start.44 = (f32[8064]{0:T(1024)}, f32[8064]{0:T(1024)}, u32[]{:S(2)}, u32[]{:S(2)}) collective-permute-start(f32[8064]{0:T(1024)} %add.4155), channel_id=1, source_target_pairs={{0,16},{8,24},{16,0},{24,8},{1,17},{9,25},{17,1},{25,9},{2,18},{10... | collective-permute-start | bytes 96776 | tf_op jit(solution)/shard_map/ppermute | solution.py:42
  432.1 27.1 %collective-permute-start.32 = (bf16[4,96,3,192]{3,1,2,0:T(8,128)(2,1)}, bf16[4,96,3,192]{3,1,2,0:T(8,128)(2,1)}, u32[]{:S(2)}, u32[]{:S(2)}) collective-permute-start(bf16[4,96,3,192]{3,1,2,0:T(8,128)(2,1)} %pad_maximum_fusion.12), channel_id=1, source_target_pairs={{0,4},{4,0},{1,5},{5,1},{2,6},{6,2},{3,7},{7,3},{8,12},{12,8},{9,1... | collective-permute-start | bytes 1327112 | tf_op jit(solution)/shard_map/ppermute | solution.py:42
  446.8 12.1 %collective-permute-start.30 = (bf16[1,256,768]{1,2,0:T(8,128)(2,1)S(1)}, bf16[1,256,768]{1,2,0:T(8,128)(2,1)S(1)}, u32[]{:S(2)}, u32[]{:S(2)}) collective-permute-start(bf16[1,256,768]{1,2,0:T(8,128)(2,1)S(1)} %fusion.149), channel_id=1, source_target_pairs={{0,2},{1,3},{2,0},{3,1},{4,6},{5,7},{6,4},{7,5},{8,10},{9,11},{10,... | collective-permute-start | bytes 1179656 | tf_op jit(solution)/shard_map/ppermute | solution.py:42
  450.3 24.9 %collective-permute-start.28 = (bf16[1,256,768]{1,2,0:T(8,128)(2,1)S(1)}, bf16[1,256,768]{1,2,0:T(8,128)(2,1)S(1)}, u32[]{:S(2)}, u32[]{:S(2)}) collective-permute-start(bf16[1,256,768]{1,2,0:T(8,128)(2,1)S(1)} %fusion.147), channel_id=1, source_target_pairs={{0,2},{1,3},{2,0},{3,1},{4,6},{5,7},{6,4},{7,5},{8,10},{9,11},{10,... | collective-permute-start | bytes 1179656 | tf_op jit(solution)/shard_map/ppermute | solution.py:42
  459.1 16.2 %collective-permute-start.31 = (bf16[256,768]{0,1:T(8,128)(2,1)S(1)}, bf16[256,768]{0,1:T(8,128)(2,1)S(1)}, u32[]{:S(2)}, u32[]{:S(2)}) collective-permute-start(bf16[256,768]{0,1:T(8,128)(2,1)S(1)} %fusion.148), channel_id=1, source_target_pairs={{0,4},{4,0},{1,5},{5,1},{2,6},{6,2},{3,7},{7,3},{8,12},{12,8},{9,1... | collective-permute-start | bytes 1179656 | tf_op jit(solution)/shard_map/ppermute | solution.py:42
  460.4 8.4 %collective-permute-start.35 = (bf16[96,3,192]{2,0,1:T(8,128)(2,1)S(1)}, bf16[96,3,192]{2,0,1:T(8,128)(2,1)S(1)}, u32[]{:S(2)}, u32[]{:S(2)}) collective-permute-start(bf16[96,3,192]{2,0,1:T(8,128)(2,1)S(1)} %get-tuple-element.296), channel_id=1, source_target_pairs={{0,24},{8,16},{16,8},{24,0},{1,25},{9,17},{17,9},{25,1},{2,26},{10... | collective-permute-start | bytes 331784 | tf_op jit(solution)/shard_map/ppermute | solution.py:42
  462.6 10.9 %collective-permute-start.34 = (bf16[96,3,192]{2,0,1:T(8,128)(2,1)S(1)}, bf16[96,3,192]{2,0,1:T(8,128)(2,1)S(1)}, u32[]{:S(2)}, u32[]{:S(2)}) collective-permute-start(bf16[96,3,192]{2,0,1:T(8,128)(2,1)S(1)} %get-tuple-element.297), channel_id=1, source_target_pairs={{0,16},{8,24},{16,0},{24,8},{1,17},{9,25},{17,1},{25,9},{2,18},{10... | collective-permute-start | bytes 331784 | tf_op jit(solution)/shard_map/ppermute | solution.py:42
  462.7 10.9 %collective-permute-start.33 = (bf16[96,3,192]{2,0,1:T(8,128)(2,1)S(1)}, bf16[96,3,192]{2,0,1:T(8,128)(2,1)S(1)}, u32[]{:S(2)}, u32[]{:S(2)}) collective-permute-start(bf16[96,3,192]{2,0,1:T(8,128)(2,1)S(1)} %get-tuple-element.295), channel_id=1, source_target_pairs={{0,8},{8,0},{16,24},{24,16},{1,9},{9,1},{17,25},{25,17},{2,10},{10... | collective-permute-start | bytes 331784 | tf_op jit(solution)/shard_map/ppermute | solution.py:42
  (183 other events, 1008.0 us)
where the time goes:
time: 491 us; the launch traced here: 482 us
  Pallas kernels  101 us (21%)
  waiting for transfers between devices  92.3 us (19%)
  local copies, waits for them, and re-layouts  91.4 us (19%)
  other arithmetic  78.7 us (16%)
  starting transfers between devices  77.6 us (16%)
  matrix products  37.8 us (8%)
    ppermute x45, waiting for transfers between devices, swap(): return lax.ppermute(values, axis, [(i, i ^ bit) for i in range(count)])  66.4 us
    ppermute x45, starting transfers between devices, swap(): return lax.ppermute(values, axis, [(i, i ^ bit) for i in range(count)])  42.1 us
    dot_general x16, matrix products, einsum(): return jnp.einsum(formula, *operands, preferred_element_type=F32)  37.8 us
    pallas_call x2, Pallas kernels, run_expert(): pl.pallas_call(functools.partial(expert_kernel, parts), grid=(steps,), ou...  33.5 us
    unnamed x372, local copies, waits for them, and re-layouts  32 us
    pallas_call x1, Pallas kernels, attend_back(): pl.pallas_call(attend_back_kernel, out_shape=(jax.ShapeDtypeStruct(querie...  29 us
    all_to_all x6, starting transfers between devices, exchange(): lax.all_to_all(values, ('dp', 'seq'), split_axis=0, concat_axis=0, tiled=...  27.7 us
    all_to_all x6, waiting for transfers between devices, exchange(): lax.all_to_all(values, ('dp', 'seq'), split_axis=0, concat_axis=0, tiled=...  25.8 us
  transfers between devices with their start and end apart: 53, of which 18 were waited for; matrix products, arithmetic and copies ran while one was open for 32% of the time, Pallas kernels for 21%

commit v1 on v0

v1 whole, which is shorter than its diff:
```python
import functools
import math

import jax
import jax.numpy as jnp
from jax import lax
from jax.experimental import pallas as pl
from jax.experimental.pallas import tpu as pltpu
from jax.sharding import PartitionSpec as P

EPSILON = 1e-06
EDGES = (1, 2, 3, 4, 5, 6, 7, 8, 12, 16, 23, 32, 46, 64, 91)
TILE = 256
HALF = TILE // 2
LOG2E = math.log2(math.e)
SCALE = 0.125
MASKED = -1e30
LOWEST = -1e29
VMEM_BYTES = 48 * 1024 * 1024
GELU_A = math.sqrt(2.0 / math.pi)
GELU_B = 0.044715
BF16 = jnp.bfloat16
F32 = jnp.float32


def dot(left_side, right_side):
    return jnp.dot(left_side, right_side, preferred_element_type=F32)


def dot_rows(left_side, right_side):
    return lax.dot_general(
        left_side, right_side, (((1,), (1,)), ((), ())), preferred_element_type=F32
    )


def einsum(formula, *operands):
    return jnp.einsum(formula, *operands, preferred_element_type=F32)


def swap(values, axis, bit):
    count = lax.axis_size(axis)
    return lax.ppermute(values, axis, [(i, i ^ bit) for i in range(count)])


def bits_of(count):
    return [1 << i for i in range(count.bit_length() - 1)]


def gather_relative(values, axis):
    pieces = {0: values}
    for bit in reversed(bits_of(lax.axis_size(axis))):
        for place in list(pieces):
            pieces[place ^ bit] = swap(pieces[place], axis, bit)
    return [pieces[place] for place in range(len(pieces))]


def sum_cores(kept, sent, axis):
    return kept.astype(F32) + swap(sent.astype(BF16), axis, 1).astype(F32)


def sum_chips(total, axis):
    bit = 2
    while bit < lax.axis_size(axis):
        pairs = total.reshape((-1, 2) + total.shape[1:])
        total = pairs[:, 0] + swap(pairs[:, 1].astype(BF16), axis, bit).astype(F32)
        bit *= 2
    return total[0]


def reorder(pieces, own_index):
    for bit in bits_of(len(pieces)):
        flip = (own_index & bit) != 0
        pieces = [
            jnp.where(flip, pieces[place ^ bit], pieces[place]) for place in range(len(pieces))
        ]
    return pieces


def gather_grid(values):
    dp_count, seq_count = lax.axis_size("dp"), lax.axis_size("seq")
    if dp_count > 4 or seq_count != 2:
        return [lax.all_gather(values, ("dp", "seq"), axis=0, tiled=True)]
    columns = [swap(values, "dp", place) for place in range(1, dp_count)]
    pieces = [values, swap(values, "seq", 1)]
    for column in columns:
        pieces += [column, swap(column, "seq", 1)]
    return pieces


def sum_all(values, axes):
    for axis in axes:
        for bit in bits_of(lax.axis_size(axis)):
            values = values + swap(values, axis, bit)
    return values


def bucket_of(relative, half_count):
    magnitude = jnp.abs(relative)
    counted = jnp.zeros(relative.shape, jnp.int32)
    for edge_value in EDGES:
        counted = counted + (magnitude >= edge_value).astype(jnp.int32)
    return counted + jnp.where(relative > 0, half_count, 0).astype(jnp.int32)


def near_buckets(half_count):
    shape = (3, HALF, HALF)
    relative = (
        (lax.broadcasted_iota(jnp.int32, shape, 0) - 1) * HALF
        + lax.broadcasted_iota(jnp.int32, shape, 1)
        - lax.broadcasted_iota(jnp.int32, shape, 2)
    )
    return bucket_of(relative, half_count)


def bias_tiles(position_bias):
    bucket_count, heads = position_bias.shape
    half_count = bucket_count // 2
    grid = near_buckets(half_count)
    near = jnp.zeros((heads, 3, HALF, HALF), F32)
    for bucket_index in range(bucket_count):
        near = near + jnp.where(
            (grid == bucket_index)[None], position_bias[bucket_index][:, None, None, None], 0.0
        )
    before, same, after = near[:, 0], near[:, 1], near[:, 2]
    far_before = jnp.broadcast_to(
        position_bias[half_count - 1][:, None, None], (heads, HALF, HALF)
    )
    far_after = jnp.broadcast_to(
        position_bias[bucket_count - 1][:, None, None], (heads, HALF, HALF)
    )

    def square(a, b, c, d):
        return jnp.concatenate(
            [jnp.concatenate([a, b], axis=2), jnp.concatenate([c, d], axis=2)], axis=1
        )

    tiles = jnp.stack(
        [
            square(far_before, far_before, far_before, far_before),
            square(far_before, far_before, before, far_before),
            square(same, before, after, same),
            square(far_after, after, far_after, far_after),
            square(far_after, far_after, far_after, far_after),
        ]
    )
    return tiles * LOG2E


def span_of(meta_ref, query_tile, key_tiles):
    opening, closing = meta_ref[1], meta_ref[2]
    first = query_tile * TILE
    last = first + TILE - 1
    begin = jnp.where(first < opening, 0, jnp.where(first < closing, opening, closing))
    end = jnp.where(last < opening, opening, jnp.where(last < closing, closing, key_tiles * TILE))
    return begin // TILE, (end + TILE - 1) // TILE


def document_of(meta_ref, tile, dimension):
    place = tile * TILE + lax.broadcasted_iota(jnp.int32, (TILE, TILE), dimension)
    return (place >= meta_ref[1]).astype(jnp.int32) + (place >= meta_ref[2]).astype(jnp.int32)


def attend_kernel(
    meta_ref,
    q_ref,
    kv_ref,
    bias_ref,
    weight_ref,
    exact_ref,
    out_ref,
    log_ref,
    even_ref,
    odd_ref,
    key_ref,
    sum_ref,
):
    key_tiles = kv_ref.shape[0]
    heads = bias_ref.shape[1]
    size = q_ref.shape[1] // heads

    def turn(tile, carry):
        for h in range(heads):
            key_ref[tile, h] = kv_ref[tile, h * size : (h + 1) * size, :].T
        return carry

    lax.fori_loop(0, key_tiles, turn, 0)

    def query_body(i, carry):
        tile = meta_ref[3 + key_tiles + i]
        place = tile % meta_ref[0]
        begin, end = span_of(meta_ref, tile, key_tiles)
        own_document = document_of(meta_ref, tile, 1)
        sum_ref[...] = jnp.zeros_like(sum_ref)

        def key_body(j, stats):
            allowed = document_of(meta_ref, j, 0) == own_document
            kind = jnp.clip(j - tile, -2, 2) + 2
            stats = list(stats)
            kept = meta_ref[3 + j]
            for h in range(heads):
                peak, total = stats[2 * h], stats[2 * h + 1]
                rows = slice(h * size, (h + 1) * size)
                scores = dot(key_ref[kept, h], q_ref[i, rows, :]) * LOG2E + bias_ref[kind, h]
                scores = jnp.where(allowed, scores, MASKED)
                new_peak = jnp.maximum(peak, jnp.max(scores, axis=0, keepdims=True))
                faded = jnp.exp2(peak - new_peak)
                weights = jnp.exp2(scores - new_peak)
                stats[2 * h] = new_peak
                stats[2 * h + 1] = total * faded + jnp.sum(weights, axis=0, keepdims=True)
                values = kv_ref[kept, (heads + h) * size : (heads + h + 1) * size, :]
                sum_ref[rows, :] = sum_ref[rows, :] * faded + dot(values, weights.astype(BF16))
            return tuple(stats)

        start = []
        for h in range(heads):
            start += [jnp.full((1, TILE), LOWEST, F32), jnp.zeros((1, TILE), F32)]
        stats = lax.fori_loop(begin, end, key_body, tuple(start))
        for h in range(heads):
            rows = slice(h * size, (h + 1) * size)
            result = sum_ref[rows, :] * (1.0 / stats[2 * h + 1])
            exact_ref[i, rows, :] = result
            out_ref[place, rows, :] = result.astype(BF16)
            log_ref[i, h] = stats[2 * h] + jnp.log2(stats[2 * h + 1])
        attended = out_ref[place]
        for k in range(weight_ref.shape[0]):
            block = dot(weight_ref[k], attended).astype(BF16)
            (odd_ref if k & 1 else even_ref)[k // 2, place] = block
        return carry

    lax.fori_loop(0, q_ref.shape[0], query_body, 0)


def estimate(queries, key_tiles, products):
    pairs = queries.shape[0] * TILE * key_tiles * TILE
    return pl.CostEstimate(
        flops=2 * products * pairs * queries.shape[1],
        bytes_accessed=8 * pairs,
        transcendentals=3 * pairs,
    )


def whole_specs(count):
    return [pl.BlockSpec(memory_space=pltpu.VMEM)] * count


def attend(meta, queries, keys_values, bias, out_blocks):
    query_tiles, width, _ = queries.shape
    key_tiles = keys_values.shape[0]
    heads = bias.shape[1]
    parts, share, _ = out_blocks.shape
    blocks = jax.ShapeDtypeStruct((parts // 2, query_tiles, share, TILE), BF16)
    return pl.pallas_call(
        attend_kernel,
        out_shape=(
            jax.ShapeDtypeStruct(queries.shape, F32),
            jax.ShapeDtypeStruct(queries.shape, BF16),
            jax.ShapeDtypeStruct((query_tiles, heads, 1, TILE), F32),
            blocks,
            blocks,
        ),
        in_specs=[pl.BlockSpec(memory_space=pltpu.SMEM)] + whole_specs(4),
        out_specs=tuple(whole_specs(5)),
        scratch_shapes=[
            pltpu.VMEM((key_tiles, heads, TILE, width // heads), BF16),
            pltpu.VMEM((width, TILE), F32),
        ],
        compiler_params=pltpu.CompilerParams(vmem_limit_bytes=VMEM_BYTES),
        cost_estimate=estimate(queries, key_tiles, 2),
        name="attend",
    )(meta, queries, keys_values, bias, out_blocks)


def bucket_rows(tiles_ref, rows_ref):
    heads, bucket_count = rows_ref.shape[:2]
    half_count = bucket_count // 2
    offset = lax.broadcasted_iota(jnp.int32, (HALF, HALF), 0) - lax.broadcasted_iota(
        jnp.int32, (HALF, HALF), 1
    )
    grids = [bucket_of(offset + shift * HALF, half_count) for shift in (-1, 0, 1)]
    first, last = slice(0, HALF), slice(HALF, TILE)

    def column_sums(values):
        return jnp.sum(values, axis=0, keepdims=True)

    def head_body(h, carry):
        before = tiles_ref[2, h, first, last] + tiles_ref[1, h, last, first]
        same = tiles_ref[2, h, first, first] + tiles_ref[2, h, last, last]
        after = tiles_ref[2, h, last, first] + tiles_ref[3, h, first, last]
        far_before = column_sums(tiles_ref[0, h, :, first] + tiles_ref[0, h, :, last])
        far_before += column_sums(tiles_ref[1, h, first, first] + tiles_ref[1, h, first, last])
        far_before += column_sums(tiles_ref[1, h, last, last])
        far_after = column_sums(tiles_ref[4, h, :, first] + tiles_ref[4, h, :, last])
        far_after += column_sums(tiles_ref[3, h, last, first] + tiles_ref[3, h, last, last])
        far_after += column_sums(tiles_ref[3, h, first, first])
        for bucket_index in range(bucket_count):
            row = column_sums(jnp.where(grids[1] == bucket_index, same, 0.0))
            if 0 < bucket_index < half_count:
                row += column_sums(jnp.where(grids[0] == bucket_index, before, 0.0))
            if bucket_index > half_count:
                row += column_sums(jnp.where(grids[2] == bucket_index, after, 0.0))
            if bucket_index == half_count - 1:
                row += far_before
            if bucket_index == bucket_count - 1:
                row += far_after
            rows_ref[h, bucket_index : bucket_index + 1, :] = row
        return carry

    lax.fori_loop(0, heads, head_body, 0)


def attend_back_kernel(
    meta_ref,
    q_ref,
    kv_ref,
    bias_ref,
    weight_ref,
    exact_ref,
    log_ref,
    *refs,
):
    parts = weight_ref.shape[0]
    branch_refs = refs[:parts]
    (
        dq_ref,
        dkv_ref,
        rows_ref,
        tiles_ref,
        key_ref,
        value_ref,
        grad_ref,
        dq_sum,
        dkv_sum,
    ) = refs[parts:]
    key_tiles = kv_ref.shape[0]
    heads = bias_ref.shape[1]
    size = q_ref.shape[1] // heads

    def turn(tile, carry):
        for h in range(heads):
            key_ref[tile, h] = kv_ref[tile, h * size : (h + 1) * size, :].T
            value_ref[tile, h] = kv_ref[tile, (heads + h) * size : (heads + h + 1) * size, :].T
        return carry

    lax.fori_loop(0, key_tiles, turn, 0)
    dkv_sum[...] = jnp.zeros_like(dkv_sum)
    tiles_ref[...] = jnp.zeros_like(tiles_ref)

    def query_body(i, carry):
        tile = meta_ref[3 + key_tiles + i]
        place = tile % meta_ref[0]
        begin, end = span_of(meta_ref, tile, key_tiles)
        own_document = document_of(meta_ref, tile, 1)
        dq_sum[...] = jnp.zeros_like(dq_sum)
        grad_sum = dot(weight_ref[0], branch_refs[0][place])
        for k in range(1, parts):
            grad_sum += dot(weight_ref[k], branch_refs[k][place])
        grad_ref[...] = grad_sum.astype(BF16)
        centres = []
        for h in range(heads):
            rows = slice(h * size, (h + 1) * size)
            centres.append(
                jnp.sum(grad_ref[rows, :].astype(F32) * exact_ref[i, rows, :], axis=0, keepdims=True)
            )

        def key_body(j, inner):
            allowed = document_of(meta_ref, j, 0) == own_document
            kept = meta_ref[3 + j]
            kind = jnp.clip(j - tile, -2, 2) + 2
            for h in range(heads):
                rows = slice(h * size, (h + 1) * size)
                value_rows = slice((heads + h) * size, (heads + h + 1) * size)
                query = q_ref[i, rows, :]
                grad = grad_ref[rows, :]
                scores = dot(key_ref[kept, h], query) * LOG2E + bias_ref[kind, h]
                probs = jnp.where(allowed, jnp.exp2(scores - log_ref[i, h]), 0.0)
                prob_grad = dot(value_ref[kept, h], grad)
                score_grad = probs * (prob_grad - centres[h])
                tiles_ref[kind, h] += score_grad
                low_grad = score_grad.astype(BF16)
                dkv_sum[kept, rows, :] += dot_rows(query, low_grad)
                dkv_sum[kept, value_rows, :] += dot_rows(grad, probs.astype(BF16))
                dq_sum[rows, :] += dot(kv_ref[kept, rows, :], low_grad)
            return inner

        lax.fori_loop(begin, end, key_body, 0)
        dq_ref[i] = (dq_sum[...] * SCALE).astype(BF16)
        return carry

    lax.fori_loop(0, q_ref.shape[0], query_body, 0)
    dkv_ref[...] = dkv_sum[...].astype(BF16)
    bucket_rows(tiles_ref, rows_ref)


def attend_back(meta, queries, keys_values, bias, out_blocks, exact, logs, branch, buckets):
    key_tiles = keys_values.shape[0]
    heads = bias.shape[1]
    size = queries.shape[1] // heads
    return pl.pallas_call(
        attend_back_kernel,
        out_shape=(
            jax.ShapeDtypeStruct(queries.shape, BF16),
            jax.ShapeDtypeStruct(keys_values.shape, BF16),
            jax.ShapeDtypeStruct((heads, buckets, HALF), F32),
        ),
        in_specs=[pl.BlockSpec(memory_space=pltpu.SMEM)] + whole_specs(6 + len(branch)),
        out_specs=tuple(whole_specs(3)),
        scratch_shapes=[
            pltpu.VMEM(bias.shape, F32),
            pltpu.VMEM((key_tiles, heads, TILE, size), BF16),
            pltpu.VMEM((key_tiles, heads, TILE, size), BF16),
            pltpu.VMEM(queries.shape[1:], BF16),
            pltpu.VMEM(queries.shape[1:], F32),
            pltpu.VMEM(keys_values.shape, F32),
        ],
        compiler_params=pltpu.CompilerParams(vmem_limit_bytes=VMEM_BYTES),
        cost_estimate=estimate(queries, key_tiles, 5),
        name="attend_back",
    )(meta, queries, keys_values, bias, out_blocks, exact, logs, *branch)


def project_kernel(piece_count, weight_count, tiles, share, own_ref, *refs):
    piece_refs = refs[:piece_count]
    weight_refs = refs[piece_count : piece_count + weight_count]
    gain_ref = refs[piece_count + weight_count]
    (
        meta_ref,
        q_ref,
        kv_ref,
        normed_ref,
        input_ref,
        in_ref,
        out_ref,
        out_t_ref,
        block_ref,
        turned_ref,
    ) = refs[piece_count + weight_count + 1 :]
    grid_place, tensor_place, seq_place, own_first = (own_ref[i] for i in range(4))
    width = gain_ref.shape[0]
    head_cols = q_ref.shape[1]
    columns = turned_ref.shape[0]
    for k in range(weight_count):
        place = grid_place ^ k if weight_count > 1 else 0
        block_ref[place] = weight_refs[k][...]
    full = block_ref[...].reshape(width, columns)
    in_ref[...] = full[:, : 3 * head_cols]
    turned_ref[...] = full.T
    blocks_here = width // share
    tall = block_ref.shape[1]
    per = share // tall if weight_count > 1 else 1
    for k in range(blocks_here):
        if weight_count > 1:
            block = block_ref[pl.ds((tensor_place ^ k) * per, per), :, 3 * head_cols :]
            block = block.reshape(share, head_cols)
        else:
            start = pl.multiple_of((tensor_place ^ k) * share, share)
            block = block_ref[0, pl.ds(start, share), 3 * head_cols :]
        out_ref[k] = block
        out_t_ref[k] = block.T
    key_tiles = kv_ref.shape[0]
    early = jnp.zeros((1, TILE), F32)
    late = jnp.zeros((1, TILE), F32)
    gain = gain_ref[...]
    turns = key_tiles // tiles
    for s in range(piece_refs[0].shape[0]):
        for k in range(piece_count):
            kept = s * piece_count + k
            rows = piece_refs[k][s, :width, :].astype(F32)
            ids = piece_refs[k][s, width : width + 16, :][:1].astype(F32)
            early += (ids < 0.5).astype(F32)
            late += (ids < 1.5).astype(F32)
            root = lax.rsqrt(jnp.sum(rows * rows, axis=0, keepdims=True) * (1.0 / width) + EPSILON)
            normed = (rows * root * gain).astype(BF16)
            normed_ref[kept] = normed
            kv_ref[kept] = dot(turned_ref[head_cols : 3 * head_cols, :], normed).astype(BF16)
    for i in range(tiles):
        normed = normed_ref[own_first + i]
        q_ref[i] = (dot(turned_ref[:head_cols, :], normed) * SCALE).astype(BF16)
        start = pl.multiple_of(tensor_place * share, share)
        if piece_count > 1:
            input_ref[tensor_place ^ i] = piece_refs[i][0, pl.ds(start, share), :]
        else:
            input_ref[i] = piece_refs[0][own_first + i, pl.ds(start, share), :]
    meta_ref[0] = tiles
    meta_ref[1] = jnp.sum(early).astype(jnp.int32)
    meta_ref[2] = jnp.sum(late).astype(jnp.int32)
    for j in range(key_tiles):
        if piece_count > 1:
            meta_ref[3 + j] = ((j // tiles) ^ seq_place) * tiles + ((j % tiles) ^ tensor_place)
        else:
            meta_ref[3 + j] = j
    for i in range(tiles):
        shift = tensor_place ^ i if piece_count > 1 else i
        meta_ref[3 + key_tiles + i] = seq_place * tiles + shift


def project(own, pieces, weight_pieces, gain, tiles, key_tiles, share):
    width = gain.shape[0]
    columns = weight_pieces[0].shape[1]
    head_cols = columns // 4
    parts = width // share
    return pl.pallas_call(
        functools.partial(project_kernel, len(pieces), len(weight_pieces), tiles, share),
        out_shape=(
            jax.ShapeDtypeStruct((3 + key_tiles + tiles,), jnp.int32),
            jax.ShapeDtypeStruct((tiles, head_cols, TILE), BF16),
            jax.ShapeDtypeStruct((key_tiles, 2 * head_cols, TILE), BF16),
            jax.ShapeDtypeStruct((key_tiles, width, TILE), BF16),
            jax.ShapeDtypeStruct((tiles, share, TILE), BF16),
            jax.ShapeDtypeStruct((width, 3 * head_cols), BF16),
            jax.ShapeDtypeStruct((parts, share, head_cols), BF16),
            jax.ShapeDtypeStruct((parts, head_cols, share), BF16),
        ),
        in_specs=[pl.BlockSpec(memory_space=pltpu.SMEM)]
        + whole_specs(len(pieces) + len(weight_pieces) + 1),
        out_specs=(pl.BlockSpec(memory_space=pltpu.SMEM),) + tuple(whole_specs(7)),
        scratch_shapes=[
            pltpu.VMEM((len(weight_pieces),) + weight_pieces[0].shape, BF16),
            pltpu.VMEM((columns, width), BF16),
        ],
        compiler_params=pltpu.CompilerParams(vmem_limit_bytes=VMEM_BYTES),
        cost_estimate=pl.CostEstimate(
            flops=6 * key_tiles * TILE * width * head_cols,
            bytes_accessed=8 * key_tiles * TILE * width,
            transcendentals=0,
        ),
        name="project",
    )(own, *pieces, *weight_pieces, gain)


def project_back_kernel(fast, parts, own_ref, dq_ref, dkv_ref, normed_ref, in_ref, attended_ref, *refs):
    branch_refs = refs[:parts]
    if fast:
        far_even, far_odd, own_even, own_odd, weight_even, weight_odd, gain_ref, full_ref = refs[
            parts:
        ]
    else:
        part_ref, weight_ref, gain_ref, full_ref = refs[parts:]
    grid_place, tensor_place, seq_place, own_first = (own_ref[i] for i in range(4))
    tiles, head_cols, _ = dq_ref.shape
    key_tiles = dkv_ref.shape[0]
    width = in_ref.shape[0]
    share = width // parts
    key_weight = in_ref[:, head_cols:]
    query_weight = in_ref[:, :head_cols]
    if fast:
        for n in range(tiles):
            block = dot(key_weight, dkv_ref[tiles + n]).astype(BF16)
            (far_odd if n & 1 else far_even)[n // 2] = block
        for n in range(tiles):
            block = dot(key_weight, dkv_ref[n]) + dot(query_weight, dq_ref[n])
            (own_odd if n & 1 else own_even)[n // 2] = block.astype(BF16)
    else:
        for n in range(key_tiles):
            part_ref[n] = dot(key_weight, dkv_ref[n]).astype(BF16)
        for n in range(tiles):
            block = part_ref[own_first + n].astype(F32) + dot(query_weight, dq_ref[n])
            part_ref[own_first + n] = block.astype(BF16)
    query_sum = dot_rows(normed_ref[own_first], dq_ref[0])
    for n in range(1, tiles):
        query_sum += dot_rows(normed_ref[own_first + n], dq_ref[n])
    key_sum = dot_rows(normed_ref[0], dkv_ref[0])
    for n in range(1, key_tiles):
        key_sum += dot_rows(normed_ref[n], dkv_ref[n])
    gain_ref[...] = jnp.sum(
        query_sum * query_weight.astype(F32), axis=1, keepdims=True
    ) + jnp.sum(key_sum * key_weight.astype(F32), axis=1, keepdims=True)
    full_ref[:, :head_cols] = query_sum.astype(BF16)
    full_ref[:, head_cols : 3 * head_cols] = key_sum.astype(BF16)
    for k in range(parts):
        block = dot_rows(branch_refs[k][0], attended_ref[0])
        for n in range(1, tiles):
            block += dot_rows(branch_refs[k][n], attended_ref[n])
        start = pl.multiple_of((tensor_place ^ k) * share, share)
        full_ref[pl.ds(start, share), 3 * head_cols :] = block.astype(BF16)
    if fast:
        tall = weight_even.shape[1]
        for k in range(weight_even.shape[0]):
            place = grid_place ^ (2 * k)
            weight_even[k] = full_ref[pl.ds(pl.multiple_of(place * tall, tall), tall), :]
            weight_odd[k] = full_ref[pl.ds(pl.multiple_of((place ^ 1) * tall, tall), tall), :]
    else:
        weight_ref[...] = full_ref[...]


def project_back(fast, own, dq, dkv, normed, in_flat, attended, branch, grid_count):
    tiles, head_cols, _ = dq.shape
    key_tiles = dkv.shape[0]
    width = in_flat.shape[0]
    parts = len(branch)
    columns = 4 * head_cols
    if fast:
        block = jax.ShapeDtypeStruct((parts // 2, width, TILE), BF16)
        weight = jax.ShapeDtypeStruct((grid_count // 2, width // grid_count, columns), BF16)
        shapes = (block,) * 4 + (weight,) * 2
    else:
        shapes = (
            jax.ShapeDtypeStruct((key_tiles, width, TILE), BF16),
            jax.ShapeDtypeStruct((width, columns), BF16),
        )
    shapes = shapes + (jax.ShapeDtypeStruct((width, 1), F32),)
    return pl.pallas_call(
        functools.partial(project_back_kernel, fast, parts),
        out_shape=shapes,
        in_specs=[pl.BlockSpec(memory_space=pltpu.SMEM)] + whole_specs(5 + parts),
        out_specs=tuple(whole_specs(len(shapes))),
        scratch_shapes=[pltpu.VMEM((width, columns), BF16)],
        compiler_params=pltpu.CompilerParams(vmem_limit_bytes=VMEM_BYTES),
        cost_estimate=pl.CostEstimate(
            flops=12 * key_tiles * TILE * width * head_cols,
            bytes_accessed=8 * key_tiles * TILE * width,
            transcendentals=0,
        ),
        name="project_back",
    )(own, dq, dkv, normed, in_flat, attended, *branch)


def finish_kernel(input_ref, gain_ref, branch_ref, result_ref, *refs):
    sum_refs = refs[:-2]
    out_ref, grad_ref = refs[-2:]
    rows = input_ref[...]
    width = rows.shape[1]
    values = rows.T
    gain = gain_ref[...]
    grad = sum_refs[0][...].astype(F32)
    for ref in sum_refs[1:]:
        grad += ref[...].astype(F32)
    root = lax.rsqrt(jnp.sum(values * values, axis=0, keepdims=True) * (1.0 / width) + EPSILON)
    scaled = grad * gain
    centre = jnp.sum(scaled * values, axis=0, keepdims=True) * (1.0 / width)
    total = root * scaled - values * (root * root * root * centre)
    grad_ref[...] = (total + branch_ref[...].astype(F32)).T
    out_ref[...] = rows + result_ref[...].astype(F32).T


def finish(block_input, gain, branch, result, sums):
    shape = jax.ShapeDtypeStruct(block_input.shape, F32)
    return pl.pallas_call(
        finish_kernel,
        out_shape=(shape, shape),
        in_specs=whole_specs(4 + len(sums)),
        out_specs=tuple(whole_specs(2)),
        compiler_params=pltpu.CompilerParams(vmem_limit_bytes=VMEM_BYTES),
        name="finish",
    )(block_input, gain, branch, result, *sums)


def split_low(values):
    high = values.astype(BF16)
    return high, (values - high.astype(F32)).astype(BF16)


def load_tile(ref, first, count, *place):
    return jnp.concatenate([ref[(first + m, *place)] for m in range(count)], axis=-1)


def expert_kernel(
    parts,
    own_ref,
    *refs,
):
    state_refs = refs[:parts]
    (grad_ref, other_ref, in_ref, in_t_ref, out_ref, router_ref, router_t_ref, gain_ref) = refs[
        parts : parts + 8
    ]
    (
        kept_ref,
        sent_ref,
        normed_ref,
        full_ref,
        act_ref,
        pre_ref,
        gate_ref,
        gain_sum,
        router_sum,
        state_ref,
        back_ref,
    ) = refs[parts + 8 :]

    @pl.when(pl.program_id(0) == 0)
    def _():
        gain_sum[...] = jnp.zeros_like(gain_sum)
        router_sum[...] = jnp.zeros_like(router_sum)

    width = gain_ref.shape[0]
    share = width // parts
    expert, own = own_ref[0], own_ref[1]
    chains, columns = state_ref.shape[0], state_ref.shape[-1]
    merged = kept_ref.shape[1] // chains
    for a in range(chains):
        for k in range(parts):
            state_ref[a, own ^ k] = load_tile(state_refs[k], a * merged, merged)
            near = 2 * (k // 2) + ((own & 1) ^ (k & 1))
            full_ref[a, near] = load_tile(
                other_ref if k & 1 else grad_ref, a * merged, merged, k // 2
            )
    for a in range(chains):
        state = state_ref[a].reshape(width, columns).astype(F32)
        root = lax.rsqrt(jnp.sum(state * state, axis=0, keepdims=True) * (1.0 / width) + EPSILON)
        gain = gain_ref[...]
        normed = (state * root * gain).astype(BF16)
        normed_ref[a] = normed
        logits = dot(router_t_ref[...], normed)
        raised = jnp.exp(logits - jnp.max(logits, axis=0, keepdims=True))
        router_probs = raised / jnp.sum(raised, axis=0, keepdims=True)
        chosen = lax.broadcasted_iota(jnp.int32, logits.shape, 0) == expert
        gate = jnp.sum(jnp.where(chosen, router_probs, 0.0), axis=0, keepdims=True)
        gate_ref[a] = gate
        act_grad = dot(out_ref[...], full_ref[a].reshape(width, columns))
        pre_act = dot(in_t_ref[...], normed)
        square = pre_act * pre_act
        bent = jnp.tanh(GELU_A * pre_act * (1.0 + GELU_B * square))
        cdf = 0.5 + 0.5 * bent
        activated = (pre_act * cdf).astype(BF16)
        act_ref[a] = activated
        slope = cdf + (0.5 * GELU_A) * pre_act * (1.0 - bent * bent) * (1.0 + (3.0 * GELU_B) * square)
        pre_grad = (act_grad * gate * slope).astype(BF16)
        pre_ref[a] = pre_grad
        gate_grad = jnp.sum(activated.astype(F32) * act_grad, axis=0, keepdims=True)
        logit_grad = gate_grad * gate * (chosen.astype(F32) - router_probs)
        high, low = split_low(logit_grad)
        router = router_ref[...]
        normed_grad = dot(in_ref[...], pre_grad) + dot(router, high) + dot(router, low)
        router_sum[...] += dot_rows(high, normed) + dot_rows(low, normed)
        plain = normed.astype(F32)
        product = normed_grad * plain
        gain_sum[...] += product
        centre = jnp.sum(product, axis=0, keepdims=True) * (1.0 / width)
        back = root * (normed_grad * gain - plain * (centre * (1.0 / gain)))
        back_ref[a] = back.astype(BF16).reshape(parts, share, columns)
        slots = columns // merged
        for k in range(parts):
            block = back_ref[a, own ^ k]
            target = sent_ref if k & 1 else kept_ref
            for m in range(merged):
                target[k // 2, a * merged + m] = block[:, m * slots : (m + 1) * slots]


def result_kernel(parts, own_ref, *refs):
    chunks = (len(refs) - 6) // 5
    sets = [refs[5 * c : 5 * c + 5] for c in range(chunks)]
    out_t_ref, kept_ref, sent_ref, in_sum, out_sum, result_ref = refs[5 * chunks :]

    @pl.when(pl.program_id(0) == 0)
    def _():
        in_sum[...] = jnp.zeros_like(in_sum)
        out_sum[...] = jnp.zeros_like(out_sum)

    own = own_ref[1]
    width = out_t_ref.shape[0]
    share = width // parts
    for c in range(chunks):
        normed_ref, full_ref, act_ref, pre_ref, gate_ref = sets[c]
        gate, activated = gate_ref[0], act_ref[0]
        columns = activated.shape[-1]
        in_sum[...] += dot_rows(normed_ref[0], pre_ref[0])
        scaled = (full_ref[0].reshape(width, columns).astype(F32) * gate).astype(BF16)
        out_sum[...] += dot_rows(activated, scaled)
        result = dot(out_t_ref[...], activated) * gate
        result_ref[...] = result.astype(BF16).reshape(parts, share, columns)
        merged = kept_ref.shape[1]
        slots = columns // merged
        for k in range(parts):
            block = result_ref[own ^ k]
            target = sent_ref if k & 1 else kept_ref
            for m in range(merged):
                target[k // 2, m, :, c * slots : (c + 1) * slots] = block[
                    :, m * slots : (m + 1) * slots
                ]


def fixed_spec(shape):
    return pl.BlockSpec(shape, lambda g: (0,) * len(shape))


def run_expert(own, states, grads, chunk, merged, chains, weights):
    parts = len(states)
    count, share, slots = states[0].shape
    width = share * parts
    columns = merged * slots
    steps = count // merged
    hidden = weights[0].shape[1]
    experts = weights[3].shape[1]
    half = parts // 2
    taken = merged * chains
    piece = pl.BlockSpec((taken, share, slots), lambda g: (g, 0, 0))
    grad_piece = pl.BlockSpec((taken, half, share, slots), lambda g: (g, 0, 0, chunk))
    split = pl.BlockSpec((half, taken, share, slots), lambda g: (0, g, 0, 0))
    wide = pl.BlockSpec((chains, width, columns), lambda g: (g, 0, 0))
    deep = pl.BlockSpec((chains, hidden, columns), lambda g: (g, 0, 0))
    tall = pl.BlockSpec((chains, parts, share, columns), lambda g: (g, 0, 0, 0))
    flat = pl.BlockSpec((chains, 1, columns), lambda g: (g, 0, 0))
    return pl.pallas_call(
        functools.partial(expert_kernel, parts),
        grid=(steps // chains,),
        out_shape=(
            jax.ShapeDtypeStruct((half, count, share, slots), BF16),
            jax.ShapeDtypeStruct((half, count, share, slots), BF16),
            jax.ShapeDtypeStruct((steps, width, columns), BF16),
            jax.ShapeDtypeStruct((steps, parts, share, columns), BF16),
            jax.ShapeDtypeStruct((steps, hidden, columns), BF16),
            jax.ShapeDtypeStruct((steps, hidden, columns), BF16),
            jax.ShapeDtypeStruct((steps, 1, columns), F32),
            jax.ShapeDtypeStruct((width, columns), F32),
            jax.ShapeDtypeStruct((experts, width), F32),
        ),
        in_specs=[pl.BlockSpec(memory_space=pltpu.SMEM)]
        + [piece] * parts
        + [grad_piece] * 2
        + [fixed_spec(weight.shape) for weight in weights],
        out_specs=(
            split,
            split,
            wide,
            tall,
            deep,
            deep,
            flat,
            fixed_spec((width, columns)),
            fixed_spec((experts, width)),
        ),
        scratch_shapes=[
            pltpu.VMEM((chains, parts, share, columns), BF16),
            pltpu.VMEM((chains, parts, share, columns), BF16),
        ],
        compiler_params=pltpu.CompilerParams(vmem_limit_bytes=VMEM_BYTES),
        cost_estimate=pl.CostEstimate(
            flops=6 * steps * columns * width * hidden,
            bytes_accessed=16 * steps * columns * width,
            transcendentals=steps * columns * hidden,
        ),
        name="expert",
    )(own, *states, *grads, *weights)


def run_result(own, saved, merged, out_t):
    chunks = len(saved)
    steps, parts, share, columns = saved[0][1].shape
    width = parts * share
    hidden = saved[0][2].shape[1]
    slots = columns // merged
    half = parts // 2
    wide = pl.BlockSpec((1, width, columns), lambda g: (g, 0, 0))
    deep = pl.BlockSpec((1, hidden, columns), lambda g: (g, 0, 0))
    tall = pl.BlockSpec((1, parts, share, columns), lambda g: (g, 0, 0, 0))
    flat = pl.BlockSpec((1, 1, columns), lambda g: (g, 0, 0))
    split = pl.BlockSpec((half, merged, share, slots * chunks), lambda g: (0, g, 0, 0))
    total = jax.ShapeDtypeStruct((half, steps * merged, share, slots * chunks), BF16)
    return pl.pallas_call(
        functools.partial(result_kernel, parts),
        grid=(steps,),
        out_shape=(
            total,
            total,
            jax.ShapeDtypeStruct((width, hidden), F32),
            jax.ShapeDtypeStruct((hidden, width), F32),
        ),
        in_specs=[pl.BlockSpec(memory_space=pltpu.SMEM)]
        + [wide, tall, deep, deep, flat] * chunks
        + [fixed_spec(out_t.shape)],
        out_specs=(split, split, fixed_spec((width, hidden)), fixed_spec((hidden, width))),
        scratch_shapes=[
            pltpu.VMEM((parts, share, columns), BF16),
        ],
        compiler_params=pltpu.CompilerParams(vmem_limit_bytes=VMEM_BYTES),
        cost_estimate=pl.CostEstimate(
            flops=6 * chunks * steps * columns * width * hidden,
            bytes_accessed=12 * chunks * steps * columns * width,
            transcendentals=0,
        ),
        name="result",
    )(own, *[array for arrays in saved for array in arrays], out_t)


def shards(
    block_input,
    attn_in_weight,
    attn_out_weight,
    position_bias,
    norm_gains,
    router_weight,
    expert_in,
    expert_out,
    segment_ids,
    expert_ids,
    out_grad,
):
    tensor_count, seq_count = lax.axis_size("tensor"), lax.axis_size("seq")
    tensor_place, seq_place = lax.axis_index("tensor"), lax.axis_index("seq")
    grid_count = lax.axis_size("dp") * seq_count
    grid_place = lax.axis_index("dp") * seq_count + seq_place
    local_count, width = block_input.shape
    group_count = local_count * tensor_count
    share = width // tensor_count
    bucket_count, heads = position_bias.shape
    head_cols = attn_in_weight.shape[2]
    experts = router_weight.shape[1]
    capacity = max(2, 2 * group_count // experts)
    tiles = group_count // TILE
    key_tiles = tiles * seq_count
    fast = seq_count == 2 and local_count == TILE and grid_count == 8

    def tiled(pieces):
        pieces = reorder(pieces, tensor_place)
        if local_count == TILE:
            return jnp.stack(pieces)
        return jnp.concatenate(pieces, axis=-1)[None]

    own_rows = jnp.concatenate(
        [
            jnp.transpose(block_input.astype(BF16)),
            jnp.pad(segment_ids.astype(BF16), ((0, 15), (0, 0))),
        ]
    )
    weight_piece = jnp.concatenate(
        [attn_in_weight[0], attn_in_weight[1], attn_in_weight[2], jnp.transpose(attn_out_weight)],
        axis=1,
    )
    if seq_count == 2:
        both_rows = jnp.stack([own_rows, swap(own_rows, "seq", 1)])
    else:
        both_rows = lax.all_gather(own_rows, "seq", axis=0, tiled=False)
    weight_pieces = gather_grid(weight_piece)
    row_pieces = gather_relative(both_rows, "tensor")
    if fast:
        own_first = jnp.int32(0)
    else:
        own_first = seq_place * tiles
        row_pieces = jnp.concatenate(reorder(row_pieces, tensor_place), axis=-1)
        if seq_count == 2:
            row_pieces = jnp.stack(reorder([row_pieces[0], row_pieces[1]], seq_place))
        row_pieces = row_pieces.reshape(seq_count, -1, tiles, TILE)
        row_pieces = [jnp.moveaxis(row_pieces, 2, 1).reshape(key_tiles, -1, TILE)]
    own = jnp.stack([grid_place, tensor_place, seq_place, own_first]).astype(jnp.int32)

    bias = bias_tiles(position_bias)
    in_t, out_t = jnp.transpose(expert_in[0]), jnp.transpose(expert_out[0])
    route_all = expert_ids[:, 0]
    expert_range = jnp.arange(experts, dtype=jnp.int32)
    route_hot = (route_all[:, None] == expert_range[None, :]).astype(jnp.int32)
    slot_rank = jnp.sum(jnp.cumsum(route_hot, axis=0) * route_hot, axis=-1) - 1
    target = (route_all * capacity + slot_rank).reshape(1, tiles, TILE, 1)
    places = jnp.arange(experts * capacity, dtype=jnp.int32).reshape(experts, 1, 1, capacity)
    onehot = (target == places).astype(BF16)
    chunks = 2 if capacity >= TILE else 1
    slots = capacity // chunks
    spread = max(1, TILE // capacity)
    merged = max(1, TILE // (slots * spread))

    def exchange(values):
        return lax.all_to_all(values, ("dp", "seq"), split_axis=0, concat_axis=0, tiled=True)

    def joined(values):
        if spread == 1:
            return values
        shape = values.shape
        values = values.reshape((-1, spread) + shape[1:])
        return jnp.moveaxis(values, 1, -2).reshape(
            (shape[0] // spread,) + shape[1:-1] + (spread * shape[-1],)
        )

    def parted(values):
        if spread == 1:
            return values
        shape = values.shape
        values = values.reshape(shape[:-1] + (spread, shape[-1] // spread))
        return jnp.moveaxis(values, -2, 1).reshape((-1,) + shape[1:-1] + (shape[-1] // spread,))

    half = tensor_count // 2
    grad_rows = jnp.transpose(out_grad.astype(BF16)).reshape(half, 2, share, local_count)
    core = tensor_place & 1
    grad_mine = lax.dynamic_index_in_dim(grad_rows, core, 1, keepdims=False)
    grad_theirs = lax.dynamic_index_in_dim(grad_rows, core ^ 1, 1, keepdims=False)
    grad_pair = jnp.stack([grad_mine, swap(grad_theirs, "tensor", 1)])
    grad_far = swap(grad_pair, "tensor", 2)
    grad_here = tiled([grad_pair[0], grad_pair[1], grad_far[0], grad_far[1]])
    grad_buffer = einsum("nkdq,enqs->ekds", grad_here, onehot).astype(BF16)

    gain_one = norm_gains[0][:, None]
    gain_two = norm_gains[1][:, None]
    gain_one, bias, in_t, out_t, target, gain_two = lax.optimization_barrier(
        (gain_one, bias, in_t, out_t, target, gain_two)
    )
    meta, queries, keys_values, normed_tiles, input_share, in_flat, out_blocks, out_t_blocks = (
        project(own, row_pieces, weight_pieces, gain_one, tiles, key_tiles, share)
    )
    queries, grad_buffer = lax.optimization_barrier((queries, grad_buffer))
    grad_arrived = joined(exchange(grad_buffer))
    exact, attended, logs, attn_even, attn_odd = attend(
        meta, queries, keys_values, bias, out_blocks
    )
    attn_share = sum_chips(sum_cores(attn_even, attn_odd, "tensor"), "tensor")
    state_share = (input_share.astype(F32) + attn_share).astype(BF16)
    state_share, grad_arrived = lax.optimization_barrier((state_share, grad_arrived))
    grad_other = swap(grad_arrived, "tensor", 1)

    weights = (
        expert_in[0],
        in_t,
        expert_out[0],
        router_weight,
        jnp.transpose(router_weight),
        gain_two,
    )
    arrivals = []
    for c in range(chunks):
        buffer = einsum("ndq,enqs->eds", state_share, onehot[..., c * slots : (c + 1) * slots])
        arrivals.append(joined(exchange(buffer.astype(BF16))))
    chains = 2 if arrivals[0].shape[0] // merged % 2 == 0 else 1
    saved, halves = [], []
    small = jnp.zeros((experts + 1, width), F32)
    for c in range(chunks):
        pieces = gather_relative(arrivals[c], "tensor")
        if halves:
            pieces[0], halves[-1] = lax.optimization_barrier((pieces[0], halves[-1]))
        kept, sent, normed_two, full, activated, pre_grad, gate, gain_sum, router_sum = run_expert(
            own, pieces, (grad_arrived, grad_other), c, merged, chains, weights
        )
        saved.append((normed_two, full, activated, pre_grad, gate))
        halves.append(sum_cores(kept, sent, "tensor"))
        gain_part = jnp.sum(gain_sum, axis=1) / norm_gains[1]
        small = small + jnp.concatenate([router_sum, gain_part[None]])
    own_late, halves[-1] = lax.optimization_barrier((own, halves[-1]))
    result_even, result_odd, grad_expert_in, grad_expert_out = run_result(
        own_late, saved, merged, out_t
    )
    state_grad = lax.dynamic_index_in_dim(grad_here, tensor_place // 2, 1, keepdims=False)
    state_grad = state_grad.astype(F32)
    for c in range(chunks):
        total = parted(sum_chips(halves[c], "tensor").astype(BF16))
        state_grad = state_grad + einsum(
            "eds,enqs->ndq", exchange(total), onehot[..., c * slots : (c + 1) * slots]
        )
    state_grad = state_grad.astype(BF16)
    result_total = sum_chips(sum_cores(result_even, result_odd, "tensor"), "tensor").astype(BF16)
    state_grad, result_total = lax.optimization_barrier((state_grad, result_total))
    result_back = exchange(parted(result_total))

    branch = gather_relative(state_grad, "tensor")
    dq, dkv, bias_rows = attend_back(
        meta, queries, keys_values, bias, out_t_blocks, exact, logs, branch, bucket_count
    )
    dq, dkv, bias_rows, result_back = lax.optimization_barrier((dq, dkv, bias_rows, result_back))

    if fast:
        far_even, far_odd, own_even, own_odd, weight_even, weight_odd, gain_part = project_back(
            True, own, dq, dkv, normed_tiles, in_flat, attended, branch, grid_count
        )
        far_half = sum_cores(far_even, far_odd, "tensor")
        own_half = sum_cores(own_even, own_odd, "tensor")
        weight_half = weight_even.astype(F32) + swap(weight_odd, "seq", 1).astype(F32)
        far_half, own_half, weight_half, small, gain_part, bias_rows, result_back = (
            lax.optimization_barrier(
                (far_half, own_half, weight_half, small, gain_part, bias_rows, result_back)
            )
        )
        far_sum = sum_chips(far_half, "tensor").astype(BF16)
        sums = [
            own_half[0],
            swap(own_half[1].astype(BF16), "tensor", 2),
            swap(far_sum, "seq", 1),
        ]
        weight_grad = weight_half[0]
        for k in range(1, grid_count // 2):
            weight_grad = weight_grad + swap(weight_half[k].astype(BF16), "dp", k).astype(F32)
    else:
        row_part, weight_part, gain_part = project_back(
            False, own, dq, dkv, normed_tiles, in_flat, attended, branch, grid_count
        )
        row_part = lax.psum_scatter(row_part, "seq", scatter_dimension=0, tiled=True)
        row_part = jnp.moveaxis(row_part, 0, 1).reshape(width, tensor_count, local_count)
        blocks = [
            lax.dynamic_index_in_dim(row_part, tensor_place ^ k, 1, keepdims=False)
            for k in range(tensor_count)
        ]
        halved = sum_cores(jnp.stack(blocks[0::2]), jnp.stack(blocks[1::2]), "tensor")
        sums = [sum_chips(halved, "tensor")]
        weight_grad = lax.psum_scatter(
            weight_part, ("dp", "seq"), scatter_dimension=0, tiled=True
        ).astype(F32)
    grad_attn_in = jnp.stack(
        [weight_grad[:, c * head_cols : (c + 1) * head_cols] for c in range(3)]
    )
    grad_attn_out = jnp.transpose(weight_grad[:, 3 * head_cols :])

    bias_padded = lax.dynamic_update_slice_in_dim(
        jnp.zeros((heads * tensor_count, bucket_count), F32),
        jnp.sum(bias_rows, axis=2),
        tensor_place * heads,
        0,
    )
    small = sum_all(
        jnp.concatenate(
            [small.reshape(-1), gain_part[:, 0] / norm_gains[0], bias_padded.reshape(-1)]
        ),
        ("tensor", "seq", "dp"),
    )
    first, second = experts * width, (experts + 1) * width
    grad_router = jnp.transpose(small[:first].reshape(experts, width))
    grad_gains = jnp.stack([small[second : second + width], small[first:second]])
    bias_sum = small[second + width :].reshape(heads * tensor_count, bucket_count)
    grad_bias = jnp.transpose(lax.dynamic_slice_in_dim(bias_sum, tensor_place * heads, heads, 0))

    result_share = attn_share + einsum("eds,enqs->ndq", result_back, onehot)
    result_share = jnp.moveaxis(result_share.astype(BF16), 0, 1).reshape(
        share, tensor_count, local_count
    )
    result_rows = lax.all_to_all(
        jnp.moveaxis(result_share, 1, 0), "tensor", split_axis=0, concat_axis=0, tiled=True
    ).reshape(width, local_count)
    if local_count == TILE:
        own_branch = [
            lax.dynamic_index_in_dim(piece, tensor_place, 0, keepdims=False) for piece in branch
        ]
    else:
        own_branch = [
            lax.dynamic_slice_in_dim(piece[0], tensor_place * local_count, local_count, 1)
            for piece in branch
        ]
    own_branch = jnp.concatenate(reorder(own_branch, tensor_place))
    block_out, input_grad = finish(block_input, gain_one, own_branch, result_rows, sums)
    return (
        block_out,
        input_grad,
        grad_attn_in,
        grad_attn_out,
        grad_bias,
        grad_gains,
        grad_router,
        grad_expert_in[None],
        grad_expert_out[None],
    )


def solution(mesh):
    return jax.shard_map(
        shards,
        mesh=mesh,
        in_specs=(
            P(("dp", "seq", "tensor"), None),
            P(None, ("dp", "seq"), "tensor"),
            P("tensor", ("dp", "seq")),
            P(None, "tensor"),
            P(),
            P(),
            P(("dp", "seq"), None, "tensor"),
            P(("dp", "seq"), "tensor", None),
            P("dp", ("seq", "tensor")),
            P(("dp", "seq"), None),
            P(("dp", "seq", "tensor"), None),
        ),
        out_specs=(
            P(("dp", "seq", "tensor"), None),
            P(("dp", "seq", "tensor"), None),
            P(None, ("dp", "seq"), "tensor"),
            P("tensor", ("dp", "seq")),
            P(None, "tensor"),
            P(),
            P(),
            P(("dp", "seq"), None, "tensor"),
            P(("dp", "seq"), "tensor", None),
        ),
        check_vma=False,
    )
```

time: 491 us -> 436 us (0.89)
  local copies, waits for them, and re-layouts: 91.4 us -> 52.8 us
  other arithmetic: 78.7 us -> 43.5 us
  matrix products: 37.8 us -> 16.7 us
  waiting for transfers between devices: 92.3 us -> 113 us
  Pallas kernels: 101 us -> 119 us
  blocking collectives: 0 us -> 15.5 us
  starting transfers between devices: 77.6 us -> 67.5 us
    ppermute x45, waiting for transfers between devices: 66.4 us -> 105 us  [swap(): return lax.ppermute(values, axis, [(i, i ^ bit) for i in range(count)])]
    dot_general x16 -> x6, matrix products: 37.8 us -> 16.7 us  [einsum(): return jnp.einsum(formula, *operands, preferred_element_type=F32)]
    all_to_all x6 -> x5, waiting for transfers between devices: 25.8 us -> 8.1 us  [exchange(): lax.all_to_all(values, ('dp', 'seq'), split_axis=0, concat_axis=0, tiled=...]
    pallas_call x2 -> x5, Pallas kernels: 33.5 us -> 50 us  [the longest x2 31.1 us: run_expert(): pl.pallas_call(functools.partial(expert_kernel, parts), grid=(steps // ch...]
    all_to_all x0 -> x1, blocking collectives: none -> 15.5 us  [exchange(): lax.all_to_all(values, ('dp', 'seq'), split_axis=0, concat_axis=0, tiled=...]
    slice x15 -> x3, local copies, waits for them, and re-layouts: 15.4 us -> 1.62 us  [the longest x2 1.34 us: shards(): small[second + width:].reshape(heads * tensor_count, bucket_count)]
    reduce_sum x13 -> x1, other arithmetic: 11.3 us -> 0.09 us  [shards(): jnp.sum(bias_rows, axis=2)]
    select_n x8 -> x0, local copies, waits for them, and re-layouts: 10.6 us -> none  [reorder(): jnp.where(flip, pieces[place ^ bit], pieces[place])]
  transfers between devices with their start and end apart: 53 -> 51, of which waited for: 18 -> 23; matrix products, arithmetic and copies ran while one was open for 32% -> 18% of each run, Pallas kernels for 21% -> 17%
where the time goes in v1:
time: 436 us; the launch traced here: 431 us
  Pallas kernels  119 us (27%)
  waiting for transfers between devices  113 us (26%)
  starting transfers between devices  67.5 us (15%)
  local copies, waits for them, and re-layouts  52.8 us (12%)
  other arithmetic  43.5 us (10%)
  matrix products  16.7 us (4%)
  blocking collectives  15.5 us (4%)
    ppermute x45, waiting for transfers between devices, swap(): return lax.ppermute(values, axis, [(i, i ^ bit) for i in range(count)])  105 us
    ppermute x45, starting transfers between devices, swap(): return lax.ppermute(values, axis, [(i, i ^ bit) for i in range(count)])  38.9 us
    unnamed x231, local copies, waits for them, and re-layouts  37.1 us
    pallas_call x2, Pallas kernels, run_expert(): pl.pallas_call(functools.partial(expert_kernel, parts), grid=(steps // ch...  31.1 us
    pallas_call x1, Pallas kernels, attend_back(): pl.pallas_call(attend_back_kernel, out_shape=(jax.ShapeDtypeStruct(querie...  29.9 us
    pallas_call x1, Pallas kernels, attend(): pl.pallas_call(attend_kernel, out_shape=(jax.ShapeDtypeStruct(queries.sha...  25.9 us
    all_to_all x5, starting transfers between devices, exchange(): lax.all_to_all(values, ('dp', 'seq'), split_axis=0, concat_axis=0, tiled=...  25.2 us
    dot_general x6, matrix products, einsum(): return jnp.einsum(formula, *operands, preferred_element_type=F32)  16.7 us
  transfers between devices with their start and end apart: 51, of which 23 were waited for; matrix products, arithmetic and copies ran while one was open for 18% of the time, Pallas kernels for 17%

profile of v1, /device:TPU:0, one launch (start us, length us, event | category | flops | bytes accessed | tf_op | source)
XLA Modules:
  0.0 430.9 jit_solution(2602042175918248982)
XLA Ops:
  2.6 5.1 %collective-permute-start.11 = (bf16[96,768]{1,0:T(8,128)(2,1)S(1)}, bf16[96,768]{1,0:T(8,128)(2,1)S(1)}, u32[]{:S(2)}, u32[]{:S(2)}) collective-permute-start(bf16[96,768]{1,0:T(8,128)(2,1)S(1)} %pad_maximum_fusion.11.refs_4_), channel_id=1, source_target_pairs={{0,24},{8,16},{16,8},{24,0},{1,25},{9,17},{17,9},{25,1},{2,26},{10... | collective-permute-start | bytes 442376 | tf_op jit(solution)/shard_map/ppermute | solution.py:42
  14.5 2.3 reduce-window.6
  19.2 2.6 select_add_fusion
  22.3 2.2 broadcast_multiply_fusion.bias_ref
  24.5 2.1 pad_maximum_fusion.4.refs_0_
  30.3 17.4 %collective-permute-done.4.refs_2_ = bf16[2,784,256]{2,1,0:T(8,128)(2,1)} collective-permute-done((bf16[2,784,256]{2,1,0:T(8,128)(2,1)}, bf16[2,784,256]{2,1,0:T(8,128)(2,1)}, u32[]{:S(2)}, u32[]{:S(2)}) %collective-permute-start.4) | collective-permute-done | bytes 802848 | tf_op jit(solution)/shard_map/ppermute | solution.py:42
  49.3 2.6 copy.40
  52.9 2.5 collective-permute-done.1
  59.2 3.0 collective-permute-done.6.refs_5_
  62.2 3.2 fusion.21
  65.5 3.0 collective-permute-done.10.refs_9_
  70.1 7.2 %project.1 = (s32[15]{0:T(128)S(1)}, bf16[4,192,256]{2,1,0:T(8,128)(2,1)S(1)}, bf16[8,384,256]{2,1,0:T(8,128)(2,1)}, bf16[8,768,256]{2,1,0:T(8,128)(2,1)}, bf16[...) custom-call(s32[4]{0:T(128)S(1)} %pad_add_fusion.own_ref, ...), custom_call_target="tpu_custom_call" | custom-call | flops 1811939328 | bytes 12582912 | tf_op jit(solution)/shard_map/project/pallas_call | solution.py:501
  80.0 4.4 %all-to-all-start = ((bf16[8,2,192,256]{3,2,1,0:T(8,128)(2,1)}), bf16[8,2,192,256]{3,2,1,0:T(8,128)(2,1)}, u32[]{:S(2)}, u32[]{:S(2)}) async-start(bf16[8,2,192,256]{3,2,1,0:T(8,128)(2,1)} %fusion.21), calls=%async_computation | async-start | bytes 3145728 | tf_op jit(solution)/shard_map/all_to_all | solution.py:950
  86.5 25.9 %attend.1 = (f32[4,192,256]{2,1,0:T(8,128)S(1)}, bf16[4,192,256]{2,1,0:T(8,128)(2,1)S(1)}, f32[4,3,1,256]{3,2,1,0:T(1,128)S(1)}, bf16[2,4,192,256]{3,2,1,0:T(8,128)(2,1)S(1)}, bf16[2,4,192,256]{3,2,1,0:T(8,128)(2,1)S(1)}) custom-call(s32[15]{0:T(128)S(1)} %copy-done.53, bf16[4,192,256]{2,1,0:T(8,128)(2,1)S(1)} %copy-done.34, ...), custom_call_target="tpu_custom_call" | custom-call | flops 1610612736 | bytes 16777216 | tf_op jit(solution)/shard_map/attend/pallas_call | solution.py:252
  112.5 2.3 collective-permute-done.13
  116.6 2.4 broadcast_compare_fusion
  119.0 7.3 %collective-permute-done.14 = bf16[1,4,192,256]{3,2,1,0:T(8,128)(2,1)S(1)} collective-permute-done((bf16[1,4,192,256]{3,2,1,0:T(8,128)(2,1)S(1)}, bf16[1,4,192,256]{3,2,1,0:T(8,128)(2,1)S(1)}, u32[]{:S(2)}, u32[]{:S(2)}) %collective-permute-start.14) | collective-permute-done | bytes 393248 | tf_op jit(solution)/shard_map/ppermute | solution.py:42
  127.2 2.2 fusion.60
  129.5 15.5 %all_to_all.35.refs_0_ = bf16[8,192,128]{2,1,0:T(8,128)(2,1)S(1)} all-to-all(bf16[8,192,128]{2,1,0:T(8,128)(2,1)S(1)} %fusion.60), channel_id=1, replica_groups=mesh['dp'=4,'seq'=2,'tensor'=4] {'dp','seq'}, dimensions={0} | all-to-all | bytes 786432 | tf_op jit(solution)/shard_map/all_to_all | solution.py:950
  146.5 8.4 %collective-permute-done.16.refs_2_ = bf16[8,192,128]{2,1,0:T(8,128)(2,1)S(1)} collective-permute-done((bf16[8,192,128]{2,1,0:T(8,128)(2,1)S(1)}, bf16[8,192,128]{2,1,0:T(8,128)(2,1)S(1)}, u32[]{:S(2)}, u32[]{:S(2)}) %collective-permute-start.16) | collective-permute-done | bytes 393248 | tf_op jit(solution)/shard_map/ppermute | solution.py:42
  156.3 4.6 %all-to-all-start.1 = ((bf16[8,192,128]{2,1,0:T(8,128)(2,1)}), bf16[8,192,128]{2,1,0:T(8,128)(2,1)S(1)}, u32[]{:S(2)}, u32[]{:S(2)}) async-start(bf16[8,192,128]{2,1,0:T(8,128)(2,1)} %fusion.63), calls=%async_computation.1 | async-start | bytes 786432 | tf_op jit(solution)/shard_map/all_to_all | solution.py:950
  167.3 15.7 %expert.2 = (bf16[2,8,192,128]{3,2,1,0:T(8,128)(2,1)S(1)}, bf16[2,8,192,128]{3,2,1,0:T(8,128)(2,1)}, bf16[4,768,256]{2,1,0:T(8,128)(2,1)}, bf16[4,4,192,256]{3,2...) custom-call(s32[4]{0:T(128)S(1)} %pad_add_fusion.own_ref, ...), custom_call_target="tpu_custom_call" | custom-call | flops 3623878656 | bytes 12582912 | tf_op jit(solution)/shard_map/expert/pallas_call | solution.py:792
  186.8 9.8 %collective-permute-done.22.refs_2_ = bf16[8,192,128]{2,1,0:T(8,128)(2,1)S(1)} collective-permute-done((bf16[8,192,128]{2,1,0:T(8,128)(2,1)S(1)}, bf16[8,192,128]{2,1,0:T(8,128)(2,1)S(1)}, u32[]{:S(2)}, u32[]{:S(2)}) %collective-permute-start.22) | collective-permute-done | bytes 393248 | tf_op jit(solution)/shard_map/ppermute | solution.py:42
  198.3 15.4 %expert.3 = (bf16[2,8,192,128]{3,2,1,0:T(8,128)(2,1)S(1)}, bf16[2,8,192,128]{3,2,1,0:T(8,128)(2,1)S(1)}, bf16[4,768,256]{2,1,0:T(8,128)(2,1)}, bf16[4,4,192,256]...) custom-call(s32[4]{0:T(128)S(1)} %pad_add_fusion.own_ref, ...), custom_call_target="tpu_custom_call" | custom-call | flops 3623878656 | bytes 12582912 | tf_op jit(solution)/shard_map/expert/pallas_call | solution.py:792
  218.5 13.3 %result.1 = (bf16[2,8,192,256]{3,2,1,0:T(8,128)(2,1)S(1)}, bf16[2,8,192,256]{3,2,1,0:T(8,128)(2,1)}, f32[768,768]{1,0:T(8,128)}, f32[768,768]{1,0:T(8,128)}) custom-call(s32[4]{0:T(128)S(1)} %pad_add_fusion.own_ref, bf16[4,768,256]{2,1,0:T(8,128)(2,1)S(1)} %copy-done.40, bf16[4,4,192,256]{3,2,1,0:T(8,128)(2,1)} %get-tuple-element.106.refs_1_, ...), custom_call_target="tpu_custom_call" | custom-call | flops 7247757312 | bytes 18874368 | tf_op jit(solution)/shard_map/result/pallas_call | solution.py:848
  235.3 9.1 %collective-permute-done.20 = bf16[1,8,192,128]{3,2,1,0:T(8,128)(2,1)S(1)} collective-permute-done((bf16[1,8,192,128]{3,2,1,0:T(8,128)(2,1)S(1)}, bf16[1,8,192,128]{3,2,1,0:T(8,128)(2,1)S(1)}, u32[]{:S(2)}, u32[]{:S(2)}) %collective-permute-start.20) | collective-permute-done | bytes 393248 | tf_op jit(solution)/shard_map/ppermute | solution.py:42
  245.2 6.0 %all-to-all-start.3 = ((bf16[8,192,128]{2,1,0:T(8,128)(2,1)}), bf16[8,192,128]{2,1,0:T(8,128)(2,1)}, u32[]{:S(2)}, u32[]{:S(2)}) async-start(bf16[8,192,128]{2,1,0:T(8,128)(2,1)} %fusion.94), calls=%async_computation.3 | async-start | bytes 786432 | tf_op jit(solution)/shard_map/all_to_all | solution.py:950
  254.2 3.5 add_bitcast_fusion
  257.7 3.9 all-to-all-done.3
  261.7 4.1 all-to-all-start.4
  268.9 3.1 fusion.42
  272.1 4.2 all-to-all-done.4
  276.2 2.6 fusion.48.refs_0_
  278.9 6.2 %collective-permute-done.27 = bf16[1,8,192,256]{3,2,1,0:T(8,128)(2,1)} collective-permute-done((bf16[1,8,192,256]{3,2,1,0:T(8,128)(2,1)S(1)}, bf16[1,8,192,256]{3,2,1,0:T(8,128)(2,1)}, u32[]{:S(2)}, u32[]{:S(2)}) %collective-permute-start.27) | collective-permute-done | bytes 786464 | tf_op jit(solution)/shard_map/ppermute | solution.py:42
  285.1 2.3 fusion.79
  287.4 6.1 %all-to-all-start.5 = ((bf16[8,192,256]{2,1,0:T(8,128)(2,1)}), bf16[8,192,256]{2,1,0:T(8,128)(2,1)}, u32[]{:S(2)}, u32[]{:S(2)}) async-start(bf16[8,192,256]{2,1,0:T(8,128)(2,1)} %fusion.79), calls=%async_computation.5 | async-start | bytes 1572864 | tf_op jit(solution)/shard_map/all_to_all | solution.py:950
  295.0 6.4 %collective-permute-done.28.refs_2_ = bf16[4,192,256]{2,1,0:T(8,128)(2,1)S(1)} collective-permute-done((bf16[4,192,256]{2,1,0:T(8,128)(2,1)S(1)}, bf16[4,192,256]{2,1,0:T(8,128)(2,1)S(1)}, u32[]{:S(2)}, u32[]{:S(2)}) %collective-permute-start.28) | collective-permute-done | bytes 393248 | tf_op jit(solution)/shard_map/ppermute | solution.py:42
  304.9 29.9 %attend_back.1 = (bf16[4,192,256]{2,1,0:T(8,128)(2,1)S(1)}, bf16[8,384,256]{2,1,0:T(8,128)(2,1)S(1)}, f32[3,32,128]{2,1,0:T(8,128)S(1)}) custom-call(s32[15]{0:T(128)S(1)} %copy-done.54, bf16[4,192,256]{2,1,0:T(8,128)(2,1)S(1)} %copy-done.35, bf16[8,384,256]{2,1,0:T(8,128)(2,1)} %get-tuple-element.87.kv_ref, ...), custom_call_target="tpu_custom_call" | custom-call | flops 4026531840 | bytes 16777216 | tf_op jit(solution)/shard_map/attend_back/pallas_call | solution.py:398
  345.6 9.7 %project_back.1 = (bf16[2,768,256]{2,1,0:T(8,128)(2,1)S(1)}, bf16[2,768,256]{2,1,0:T(8,128)(2,1)S(1)}, bf16[2,768,256]{2,1,0:T(8,128)(2,1)}, bf16[2,768,256]{2,1...) custom-call(s32[4]{0:T(128)S(1)} %pad_add_fusion.own_ref, ...), custom_call_target="tpu_custom_call" | custom-call | flops 3623878656 | bytes 12582912 | tf_op jit(solution)/shard_map/project_back/pallas_call | solution.py:601
  361.3 12.2 %collective-permute-done.33 = bf16[4,96,768]{2,1,0:T(8,128)(2,1)} collective-permute-done((bf16[4,96,768]{2,1,0:T(8,128)(2,1)}, bf16[4,96,768]{2,1,0:T(8,128)(2,1)}, u32[]{:S(2)}, u32[]{:S(2)}) %collective-permute-start.33) | collective-permute-done | bytes 589856 | tf_op jit(solution)/shard_map/ppermute | solution.py:42
  373.5 2.2 convert_add_fusion.4
  379.1 4.0 fusion.51
  385.6 3.5 all-to-all-start.6
  394.4 2.9 collective-permute-start.43
  400.5 2.9 collective-permute-done.43
  412.7 4.7 %collective-permute-done.35 = bf16[1,768,256]{2,1,0:T(8,128)(2,1)} collective-permute-done((bf16[1,768,256]{2,1,0:T(8,128)(2,1)S(1)}, bf16[1,768,256]{2,1,0:T(8,128)(2,1)}, u32[]{:S(2)}, u32[]{:S(2)}) %collective-permute-start.35) | collective-permute-done | bytes 393248 | tf_op jit(solution)/shard_map/ppermute | solution.py:42
  417.3 2.1 fusion.99
  425.7 3.2 collective-permute-done.36.refs_2_
  (392 shorter events, 113.5 us)
Async XLA Ops:
  2.6 49.5 %collective-permute-start.11 = (bf16[96,768]{1,0:T(8,128)(2,1)S(1)}, bf16[96,768]{1,0:T(8,128)(2,1)S(1)}, u32[]{:S(2)}, u32[]{:S(2)}) collective-permute-start(bf16[96,768]{1,0:T(8,128)(2,1)S(1)} %pad_maximum_fusion.11.refs_4_), channel_id=1, source_target_pairs={{0,24},{8,16},{16,8},{24,0},{1,25},{9,17},{17,9},{25,1},{2,26},{10... | collective-permute-start | bytes 442376 | tf_op jit(solution)/shard_map/ppermute | solution.py:42
  7.7 49.3 %collective-permute-start.9 = (bf16[96,768]{1,0:T(8,128)(2,1)S(1)}, bf16[96,768]{1,0:T(8,128)(2,1)S(1)}, u32[]{:S(2)}, u32[]{:S(2)}) collective-permute-start(bf16[96,768]{1,0:T(8,128)(2,1)S(1)} %pad_maximum_fusion.11.refs_4_), channel_id=1, source_target_pairs={{0,16},{8,24},{16,0},{24,8},{1,17},{9,25},{17,1},{25,9},{2,18},{10... | collective-permute-start | bytes 442376 | tf_op jit(solution)/shard_map/ppermute | solution.py:42
  9.8 19.0 %collective-permute-start = (bf16[2,192,256]{2,1,0:T(8,128)(2,1)}, bf16[2,192,256]{2,1,0:T(8,128)(2,1)S(1)}, u32[]{:S(2)}, u32[]{:S(2)}) collective-permute-start(bf16[2,192,256]{2,1,0:T(8,128)(2,1)} %get-tuple-element.222), channel_id=1, source_target_pairs={{0,1},{1,0},{2,3},{3,2},{4,5},{5,4},{6,7},{7,6},{8,9},{9,8},{10,11... | collective-permute-start | bytes 589832 | tf_op jit(solution)/shard_map/ppermute | solution.py:42
  11.0 13.5 %collective-permute-start.2 = (bf16[784,256]{1,0:T(8,128)(2,1)}, bf16[784,256]{1,0:T(8,128)(2,1)}, u32[]{:S(2)}, u32[]{:S(2)}) collective-permute-start(bf16[784,256]{1,0:T(8,128)(2,1)} %get-tuple-element.220), channel_id=1, source_target_pairs={{0,4},{4,0},{1,5},{5,1},{2,6},{6,2},{3,7},{7,3},{8,12},{12,8},{9,1... | collective-permute-start | bytes 1204232 | tf_op jit(solution)/shard_map/ppermute | solution.py:42
  26.7 21.0 %collective-permute-start.4 = (bf16[2,784,256]{2,1,0:T(8,128)(2,1)}, bf16[2,784,256]{2,1,0:T(8,128)(2,1)}, u32[]{:S(2)}, u32[]{:S(2)}) collective-permute-start(bf16[2,784,256]{2,1,0:T(8,128)(2,1)} %pad_maximum_fusion.4.refs_0_), channel_id=1, source_target_pairs={{0,2},{1,3},{2,0},{3,1},{4,6},{5,7},{6,4},{7,5},{8,10},{9,11},{10,... | collective-permute-start | bytes 2408456 | tf_op jit(solution)/shard_map/ppermute | solution.py:42
  29.6 25.8 %collective-permute-start.1 = (bf16[2,2,192,256]{3,2,1,0:T(8,128)(2,1)}, bf16[2,2,192,256]{3,2,1,0:T(8,128)(2,1)}, u32[]{:S(2)}, u32[]{:S(2)}) collective-permute-start(bf16[2,2,192,256]{3,2,1,0:T(8,128)(2,1)} %pad_maximum_fusion.8), channel_id=1, source_target_pairs={{0,2},{1,3},{2,0},{3,1},{4,6},{5,7},{6,4},{7,5},{8,10},{9,11},{10,... | collective-permute-start | bytes 1179656 | tf_op jit(solution)/shard_map/ppermute | solution.py:42
  30.2 39.9 %collective-permute-start.3 = (bf16[2,784,256]{2,1,0:T(8,128)(2,1)}, bf16[2,784,256]{2,1,0:T(8,128)(2,1)}, u32[]{:S(2)}, u32[]{:S(2)}) collective-permute-start(bf16[2,784,256]{2,1,0:T(8,128)(2,1)} %pad_maximum_fusion.4.refs_0_), channel_id=1, source_target_pairs={{0,1},{1,0},{2,3},{3,2},{4,5},{5,4},{6,7},{7,6},{8,9},{9,8},{10,11... | collective-permute-start | bytes 2408456 | tf_op jit(solution)/shard_map/ppermute | solution.py:42
  47.7 22.4 %collective-permute-start.5 = (bf16[2,784,256]{2,1,0:T(8,128)(2,1)}, bf16[2,784,256]{2,1,0:T(8,128)(2,1)}, u32[]{:S(2)}, u32[]{:S(2)}) collective-permute-start(bf16[2,784,256]{2,1,0:T(8,128)(2,1)} %collective-permute-done.4.refs_2_), channel_id=1, source_target_pairs={{0,1},{1,0},{2,3},{3,2},{4,5},{5,4},{6,7},{7,6},{8,9},{9,8},{10,11... | collective-permute-start | bytes 2408456 | tf_op jit(solution)/shard_map/ppermute | solution.py:42
  52.1 6.6 %collective-permute-start.7 = (bf16[96,768]{1,0:T(8,128)(2,1)S(1)}, bf16[96,768]{1,0:T(8,128)(2,1)S(1)}, u32[]{:S(2)}, u32[]{:S(2)}) collective-permute-start(bf16[96,768]{1,0:T(8,128)(2,1)S(1)} %pad_maximum_fusion.11.refs_4_), channel_id=1, source_target_pairs={{0,8},{8,0},{16,24},{24,16},{1,9},{9,1},{17,25},{25,17},{2,10},{10... | collective-permute-start | bytes 442376 | tf_op jit(solution)/shard_map/ppermute | solution.py:42
  55.4 6.8 %collective-permute-start.6 = (bf16[96,768]{1,0:T(8,128)(2,1)S(1)}, bf16[96,768]{1,0:T(8,128)(2,1)S(1)}, u32[]{:S(2)}, u32[]{:S(2)}) collective-permute-start(bf16[96,768]{1,0:T(8,128)(2,1)S(1)} %pad_maximum_fusion.11.refs_4_), channel_id=1, source_target_pairs={{0,4},{4,0},{1,5},{5,1},{2,6},{6,2},{3,7},{7,3},{8,12},{12,8},{9,1... | collective-permute-start | bytes 442376 | tf_op jit(solution)/shard_map/ppermute | solution.py:42
  57.1 8.4 %collective-permute-start.12 = (bf16[96,768]{1,0:T(8,128)(2,1)S(1)}, bf16[96,768]{1,0:T(8,128)(2,1)S(1)}, u32[]{:S(2)}, u32[]{:S(2)}) collective-permute-start(bf16[96,768]{1,0:T(8,128)(2,1)S(1)} %collective-permute-done.11.refs_10_), channel_id=1, source_target_pairs={{0,4},{4,0},{1,5},{5,1},{2,6},{6,2},{3,7},{7,3},{8,12},{12,8},{9,1... | collective-permute-start | bytes 442376 | tf_op jit(solution)/shard_map/ppermute | solution.py:42
  58.7 9.8 %collective-permute-start.10 = (bf16[96,768]{1,0:T(8,128)(2,1)S(1)}, bf16[96,768]{1,0:T(8,128)(2,1)S(1)}, u32[]{:S(2)}, u32[]{:S(2)}) collective-permute-start(bf16[96,768]{1,0:T(8,128)(2,1)S(1)} %collective-permute-done.9.refs_8_), channel_id=1, source_target_pairs={{0,4},{4,0},{1,5},{5,1},{2,6},{6,2},{3,7},{7,3},{8,12},{12,8},{9,1... | collective-permute-start | bytes 442376 | tf_op jit(solution)/shard_map/ppermute | solution.py:42
  62.2 7.8 %collective-permute-start.8 = (bf16[96,768]{1,0:T(8,128)(2,1)S(1)}, bf16[96,768]{1,0:T(8,128)(2,1)S(1)}, u32[]{:S(2)}, u32[]{:S(2)}) collective-permute-start(bf16[96,768]{1,0:T(8,128)(2,1)S(1)} %collective-permute-done.7.refs_6_), channel_id=1, source_target_pairs={{0,4},{4,0},{1,5},{5,1},{2,6},{6,2},{3,7},{7,3},{8,12},{12,8},{9,1... | collective-permute-start | bytes 442376 | tf_op jit(solution)/shard_map/ppermute | solution.py:42
  80.0 47.2 %all-to-all-start = ((bf16[8,2,192,256]{3,2,1,0:T(8,128)(2,1)}), bf16[8,2,192,256]{3,2,1,0:T(8,128)(2,1)}, u32[]{:S(2)}, u32[]{:S(2)}) async-start(bf16[8,2,192,256]{3,2,1,0:T(8,128)(2,1)} %fusion.21), calls=%async_computation | async-start | bytes 3145728 | tf_op jit(solution)/shard_map/all_to_all | solution.py:950
  115.1 11.2 %collective-permute-start.14 = (bf16[1,4,192,256]{3,2,1,0:T(8,128)(2,1)S(1)}, bf16[1,4,192,256]{3,2,1,0:T(8,128)(2,1)S(1)}, u32[]{:S(2)}, u32[]{:S(2)}) collective-permute-start(bf16[1,4,192,256]{3,2,1,0:T(8,128)(2,1)S(1)} %fusion.93), channel_id=1, source_target_pairs={{0,2},{1,3},{2,0},{3,1},{4,6},{5,7},{6,4},{7,5},{8,10},{9,11},{10,... | collective-permute-start | bytes 1179656 | tf_op jit(solution)/shard_map/ppermute | solution.py:42
  127.2 36.1 %collective-permute-start.18 = (bf16[8,2,192,256]{3,2,1,0:T(8,128)(2,1)}, bf16[8,2,192,256]{3,2,1,0:T(8,128)(2,1)}, u32[]{:S(2)}, u32[]{:S(2)}) collective-permute-start(bf16[8,2,192,256]{3,2,1,0:T(8,128)(2,1)} %all-to-all-done.refs_4_), channel_id=1, source_target_pairs={{0,1},{1,0},{2,3},{3,2},{4,5},{5,4},{6,7},{7,6},{8,9},{9,8},{10,11... | collective-permute-start | bytes 4718600 | tf_op jit(solution)/shard_map/ppermute | solution.py:42
  145.0 9.9 %collective-permute-start.16 = (bf16[8,192,128]{2,1,0:T(8,128)(2,1)S(1)}, bf16[8,192,128]{2,1,0:T(8,128)(2,1)S(1)}, u32[]{:S(2)}, u32[]{:S(2)}) collective-permute-start(bf16[8,192,128]{2,1,0:T(8,128)(2,1)S(1)} %all_to_all.35.refs_0_), channel_id=1, source_target_pairs={{0,2},{1,3},{2,0},{3,1},{4,6},{5,7},{6,4},{7,5},{8,10},{9,11},{10,... | collective-permute-start | bytes 1179656 | tf_op jit(solution)/shard_map/ppermute | solution.py:42
  146.5 16.9 %collective-permute-start.15 = (bf16[8,192,128]{2,1,0:T(8,128)(2,1)S(1)}, bf16[8,192,128]{2,1,0:T(8,128)(2,1)}, u32[]{:S(2)}, u32[]{:S(2)}) collective-permute-start(bf16[8,192,128]{2,1,0:T(8,128)(2,1)S(1)} %all_to_all.35.refs_0_), channel_id=1, source_target_pairs={{0,1},{1,0},{2,3},{3,2},{4,5},{5,4},{6,7},{7,6},{8,9},{9,8},{10,11... | collective-permute-start | bytes 1179656 | tf_op jit(solution)/shard_map/ppermute | solution.py:42
  154.9 8.5 %collective-permute-start.17 = (bf16[8,192,128]{2,1,0:T(8,128)(2,1)S(1)}, bf16[8,192,128]{2,1,0:T(8,128)(2,1)}, u32[]{:S(2)}, u32[]{:S(2)}) collective-permute-start(bf16[8,192,128]{2,1,0:T(8,128)(2,1)S(1)} %collective-permute-done.16.refs_2_), channel_id=1, source_target_pairs={{0,1},{1,0},{2,3},{3,2},{4,5},{5,4},{6,7},{7,6},{8,9},{9,8},{10,11... | collective-permute-start | bytes 1179656 | tf_op jit(solution)/shard_map/ppermute | solution.py:42
  156.3 28.9 %all-to-all-start.1 = ((bf16[8,192,128]{2,1,0:T(8,128)(2,1)}), bf16[8,192,128]{2,1,0:T(8,128)(2,1)S(1)}, u32[]{:S(2)}, u32[]{:S(2)}) async-start(bf16[8,192,128]{2,1,0:T(8,128)(2,1)} %fusion.63), calls=%async_computation.1 | async-start | bytes 786432 | tf_op jit(solution)/shard_map/all_to_all | solution.py:950
  185.0 11.5 %collective-permute-start.19 = (bf16[2,8,192,128]{3,2,1,0:T(8,128)(2,1)}, bf16[2,8,192,128]{3,2,1,0:T(8,128)(2,1)}, u32[]{:S(2)}, u32[]{:S(2)}) collective-permute-start(bf16[2,8,192,128]{3,2,1,0:T(8,128)(2,1)} %get-tuple-element.98), channel_id=1, source_target_pairs={{0,1},{1,0},{2,3},{3,2},{4,5},{5,4},{6,7},{7,6},{8,9},{9,8},{10,11... | collective-permute-start | bytes 2359304 | tf_op jit(solution)/shard_map/ppermute | solution.py:42
  185.2 11.3 %collective-permute-start.22 = (bf16[8,192,128]{2,1,0:T(8,128)(2,1)S(1)}, bf16[8,192,128]{2,1,0:T(8,128)(2,1)S(1)}, u32[]{:S(2)}, u32[]{:S(2)}) collective-permute-start(bf16[8,192,128]{2,1,0:T(8,128)(2,1)S(1)} %all-to-all-done.1.refs_0_), channel_id=1, source_target_pairs={{0,2},{1,3},{2,0},{3,1},{4,6},{5,7},{6,4},{7,5},{8,10},{9,11},{10,... | collective-permute-start | bytes 1179656 | tf_op jit(solution)/shard_map/ppermute | solution.py:42
  186.7 11.5 %collective-permute-start.21 = (bf16[8,192,128]{2,1,0:T(8,128)(2,1)S(1)}, bf16[8,192,128]{2,1,0:T(8,128)(2,1)S(1)}, u32[]{:S(2)}, u32[]{:S(2)}) collective-permute-start(bf16[8,192,128]{2,1,0:T(8,128)(2,1)S(1)} %all-to-all-done.1.refs_0_), channel_id=1, source_target_pairs={{0,1},{1,0},{2,3},{3,2},{4,5},{5,4},{6,7},{7,6},{8,9},{9,8},{10,11... | collective-permute-start | bytes 1179656 | tf_op jit(solution)/shard_map/ppermute | solution.py:42
  213.7 2.5 collective-permute-start.24
  231.9 22.3 %collective-permute-start.26 = (bf16[2,8,192,256]{3,2,1,0:T(8,128)(2,1)}, bf16[2,8,192,256]{3,2,1,0:T(8,128)(2,1)}, u32[]{:S(2)}, u32[]{:S(2)}) collective-permute-start(bf16[2,8,192,256]{3,2,1,0:T(8,128)(2,1)} %get-tuple-element.117), channel_id=1, source_target_pairs={{0,1},{1,0},{2,3},{3,2},{4,5},{5,4},{6,7},{7,6},{8,9},{9,8},{10,11... | collective-permute-start | bytes 4718600 | tf_op jit(solution)/shard_map/ppermute | solution.py:42
  232.4 12.0 %collective-permute-start.20 = (bf16[1,8,192,128]{3,2,1,0:T(8,128)(2,1)S(1)}, bf16[1,8,192,128]{3,2,1,0:T(8,128)(2,1)S(1)}, u32[]{:S(2)}, u32[]{:S(2)}) collective-permute-start(bf16[1,8,192,128]{3,2,1,0:T(8,128)(2,1)S(1)} %fusion.95), channel_id=1, source_target_pairs={{0,2},{1,3},{2,0},{3,1},{4,6},{5,7},{6,4},{7,5},{8,10},{9,11},{10,... | collective-permute-start | bytes 1179656 | tf_op jit(solution)/shard_map/ppermute | solution.py:42
  234.7 17.4 %collective-permute-start.25 = (bf16[1,8,192,128]{3,2,1,0:T(8,128)(2,1)}, bf16[1,8,192,128]{3,2,1,0:T(8,128)(2,1)}, u32[]{:S(2)}, u32[]{:S(2)}) collective-permute-start(bf16[1,8,192,128]{3,2,1,0:T(8,128)(2,1)} %fusion.97), channel_id=1, source_target_pairs={{0,2},{1,3},{2,0},{3,1},{4,6},{5,7},{6,4},{7,5},{8,10},{9,11},{10,... | collective-permute-start | bytes 1179656 | tf_op jit(solution)/shard_map/ppermute | solution.py:42
  245.2 16.4 %all-to-all-start.3 = ((bf16[8,192,128]{2,1,0:T(8,128)(2,1)}), bf16[8,192,128]{2,1,0:T(8,128)(2,1)}, u32[]{:S(2)}, u32[]{:S(2)}) async-start(bf16[8,192,128]{2,1,0:T(8,128)(2,1)} %fusion.94), calls=%async_computation.3 | async-start | bytes 786432 | tf_op jit(solution)/shard_map/all_to_all | solution.py:950
  261.7 14.6 %all-to-all-start.4 = ((bf16[8,192,128]{2,1,0:T(8,128)(2,1)}), bf16[8,192,128]{2,1,0:T(8,128)(2,1)}, u32[]{:S(2)}, u32[]{:S(2)}) async-start(bf16[8,192,128]{2,1,0:T(8,128)(2,1)} %fusion.96), calls=%async_computation.4 | async-start | bytes 786432 | tf_op jit(solution)/shard_map/all_to_all | solution.py:950
  267.3 17.9 %collective-permute-start.27 = (bf16[1,8,192,256]{3,2,1,0:T(8,128)(2,1)S(1)}, bf16[1,8,192,256]{3,2,1,0:T(8,128)(2,1)}, u32[]{:S(2)}, u32[]{:S(2)}) collective-permute-start(bf16[1,8,192,256]{3,2,1,0:T(8,128)(2,1)S(1)} %fusion.80), channel_id=1, source_target_pairs={{0,2},{1,3},{2,0},{3,1},{4,6},{5,7},{6,4},{7,5},{8,10},{9,11},{10,... | collective-permute-start | bytes 2359304 | tf_op jit(solution)/shard_map/ppermute | solution.py:42
  287.4 52.2 %all-to-all-start.5 = ((bf16[8,192,256]{2,1,0:T(8,128)(2,1)}), bf16[8,192,256]{2,1,0:T(8,128)(2,1)}, u32[]{:S(2)}, u32[]{:S(2)}) async-start(bf16[8,192,256]{2,1,0:T(8,128)(2,1)} %fusion.79), calls=%async_computation.5 | async-start | bytes 1572864 | tf_op jit(solution)/shard_map/all_to_all | solution.py:950
  293.5 7.9 %collective-permute-start.28 = (bf16[4,192,256]{2,1,0:T(8,128)(2,1)S(1)}, bf16[4,192,256]{2,1,0:T(8,128)(2,1)S(1)}, u32[]{:S(2)}, u32[]{:S(2)}) collective-permute-start(bf16[4,192,256]{2,1,0:T(8,128)(2,1)S(1)} %fusion.48.refs_0_), channel_id=1, source_target_pairs={{0,2},{1,3},{2,0},{3,1},{4,6},{5,7},{6,4},{7,5},{8,10},{9,11},{10,... | collective-permute-start | bytes 1179656 | tf_op jit(solution)/shard_map/ppermute | solution.py:42
  295.0 6.4 %collective-permute-start.30 = (bf16[4,192,256]{2,1,0:T(8,128)(2,1)S(1)}, bf16[4,192,256]{2,1,0:T(8,128)(2,1)S(1)}, u32[]{:S(2)}, u32[]{:S(2)}) collective-permute-start(bf16[4,192,256]{2,1,0:T(8,128)(2,1)S(1)} %fusion.48.refs_0_), channel_id=1, source_target_pairs={{0,1},{1,0},{2,3},{3,2},{4,5},{5,4},{6,7},{7,6},{8,9},{9,8},{10,11... | collective-permute-start | bytes 1179656 | tf_op jit(solution)/shard_map/ppermute | solution.py:42
  357.8 15.7 %collective-permute-start.33 = (bf16[4,96,768]{2,1,0:T(8,128)(2,1)}, bf16[4,96,768]{2,1,0:T(8,128)(2,1)}, u32[]{:S(2)}, u32[]{:S(2)}) collective-permute-start(bf16[4,96,768]{2,1,0:T(8,128)(2,1)} %get-tuple-element.136), channel_id=1, source_target_pairs={{0,4},{4,0},{1,5},{5,1},{2,6},{6,2},{3,7},{7,3},{8,12},{12,8},{9,1... | collective-permute-start | bytes 1769480 | tf_op jit(solution)/shard_map/ppermute | solution.py:42
  358.2 17.5 %collective-permute-start.31 = (bf16[2,768,256]{2,1,0:T(8,128)(2,1)}, bf16[2,768,256]{2,1,0:T(8,128)(2,1)S(1)}, u32[]{:S(2)}, u32[]{:S(2)}) collective-permute-start(bf16[2,768,256]{2,1,0:T(8,128)(2,1)} %copy-done.29), channel_id=1, source_target_pairs={{0,1},{1,0},{2,3},{3,2},{4,5},{5,4},{6,7},{7,6},{8,9},{9,8},{10,11... | collective-permute-start | bytes 2359304 | tf_op jit(solution)/shard_map/ppermute | solution.py:42
  359.9 17.1 %collective-permute-start.32 = (bf16[2,768,256]{2,1,0:T(8,128)(2,1)}, bf16[2,768,256]{2,1,0:T(8,128)(2,1)S(1)}, u32[]{:S(2)}, u32[]{:S(2)}) collective-permute-start(bf16[2,768,256]{2,1,0:T(8,128)(2,1)} %get-tuple-element.134), channel_id=1, source_target_pairs={{0,1},{1,0},{2,3},{3,2},{4,5},{5,4},{6,7},{7,6},{8,9},{9,8},{10,11... | collective-permute-start | bytes 2359304 | tf_op jit(solution)/shard_map/ppermute | solution.py:42
  379.0 4.2 collective-permute-start.40
  383.2 7.2 %collective-permute-start.41 = (f32[8064]{0:T(1024)S(1)}, f32[8064]{0:T(1024)S(1)}, u32[]{:S(2)}, u32[]{:S(2)}) collective-permute-start(f32[8064]{0:T(1024)S(1)} %fusion.133), channel_id=1, source_target_pairs={{0,2},{1,3},{2,0},{3,1},{4,6},{5,7},{6,4},{7,5},{8,10},{9,11},{10,... | collective-permute-start | bytes 96776 | tf_op jit(solution)/shard_map/ppermute | solution.py:42
  385.6 40.1 %all-to-all-start.6 = ((bf16[4,192,256]{2,1,0:T(8,128)(2,1)}), bf16[4,192,256]{2,1,0:T(8,128)(2,1)S(1)}, u32[]{:S(2)}, u32[]{:S(2)}) async-start(bf16[4,192,256]{2,1,0:T(8,128)(2,1)} %fusion.51), calls=%async_computation.6 | async-start | bytes 786432 | tf_op jit(solution)/shard_map/all_to_all | solution.py:1107
  390.4 4.0 collective-permute-start.42
  390.8 14.9 %collective-permute-start.37 = (bf16[96,768]{1,0:T(8,128)(2,1)S(1)}, bf16[96,768]{1,0:T(8,128)(2,1)S(1)}, u32[]{:S(2)}, u32[]{:S(2)}) collective-permute-start(bf16[96,768]{1,0:T(8,128)(2,1)S(1)} %get-tuple-element.213), channel_id=1, source_target_pairs={{0,8},{8,0},{16,24},{24,16},{1,9},{9,1},{17,25},{25,17},{2,10},{10... | collective-permute-start | bytes 442376 | tf_op jit(solution)/shard_map/ppermute | solution.py:42
  392.8 14.2 %collective-permute-start.39 = (bf16[96,768]{1,0:T(8,128)(2,1)S(1)}, bf16[96,768]{1,0:T(8,128)(2,1)S(1)}, u32[]{:S(2)}, u32[]{:S(2)}) collective-permute-start(bf16[96,768]{1,0:T(8,128)(2,1)S(1)} %get-tuple-element.214), channel_id=1, source_target_pairs={{0,24},{8,16},{16,8},{24,0},{1,25},{9,17},{17,9},{25,1},{2,26},{10... | collective-permute-start | bytes 442376 | tf_op jit(solution)/shard_map/ppermute | solution.py:42
  392.8 15.0 %collective-permute-start.38 = (bf16[96,768]{1,0:T(8,128)(2,1)S(1)}, bf16[96,768]{1,0:T(8,128)(2,1)S(1)}, u32[]{:S(2)}, u32[]{:S(2)}) collective-permute-start(bf16[96,768]{1,0:T(8,128)(2,1)S(1)} %get-tuple-element.215), channel_id=1, source_target_pairs={{0,16},{8,24},{16,0},{24,8},{1,17},{9,25},{17,1},{25,9},{2,18},{10... | collective-permute-start | bytes 442376 | tf_op jit(solution)/shard_map/ppermute | solution.py:42
  394.4 9.0 %collective-permute-start.43 = (f32[8064]{0:T(1024)S(1)}, f32[8064]{0:T(1024)S(1)}, u32[]{:S(2)}, u32[]{:S(2)}) collective-permute-start(f32[8064]{0:T(1024)S(1)} %add.2891), channel_id=1, source_target_pairs={{0,8},{8,0},{16,24},{24,16},{1,9},{9,1},{17,25},{25,17},{2,10},{10... | collective-permute-start | bytes 96776 | tf_op jit(solution)/shard_map/ppermute | solution.py:42
  398.4 27.3 %collective-permute-start.34 = (bf16[768,256]{1,0:T(8,128)(2,1)}, bf16[768,256]{1,0:T(8,128)(2,1)S(1)}, u32[]{:S(2)}, u32[]{:S(2)}) collective-permute-start(bf16[768,256]{1,0:T(8,128)(2,1)} %fusion.98), channel_id=1, source_target_pairs={{0,2},{1,3},{2,0},{3,1},{4,6},{5,7},{6,4},{7,5},{8,10},{9,11},{10,... | collective-permute-start | bytes 1179656 | tf_op jit(solution)/shard_map/ppermute | solution.py:42
  403.4 14.0 %collective-permute-start.35 = (bf16[1,768,256]{2,1,0:T(8,128)(2,1)S(1)}, bf16[1,768,256]{2,1,0:T(8,128)(2,1)}, u32[]{:S(2)}, u32[]{:S(2)}) collective-permute-start(bf16[1,768,256]{2,1,0:T(8,128)(2,1)S(1)} %fusion.100), channel_id=1, source_target_pairs={{0,2},{1,3},{2,0},{3,1},{4,6},{5,7},{6,4},{7,5},{8,10},{9,11},{10,... | collective-permute-start | bytes 1179656 | tf_op jit(solution)/shard_map/ppermute | solution.py:42
  405.6 6.2 %collective-permute-start.44 = (f32[8064]{0:T(1024)}, f32[8064]{0:T(1024)}, u32[]{:S(2)}, u32[]{:S(2)}) collective-permute-start(f32[8064]{0:T(1024)} %add.2892), channel_id=1, source_target_pairs={{0,16},{8,24},{16,0},{24,8},{1,17},{9,25},{17,1},{25,9},{2,18},{10... | collective-permute-start | bytes 96776 | tf_op jit(solution)/shard_map/ppermute | solution.py:42
  419.4 9.4 %collective-permute-start.36 = (bf16[768,256]{1,0:T(8,128)(2,1)}, bf16[768,256]{1,0:T(8,128)(2,1)S(1)}, u32[]{:S(2)}, u32[]{:S(2)}) collective-permute-start(bf16[768,256]{1,0:T(8,128)(2,1)} %fusion.99), channel_id=1, source_target_pairs={{0,4},{4,0},{1,5},{5,1},{2,6},{6,2},{3,7},{7,3},{8,12},{12,8},{9,1... | collective-permute-start | bytes 1179656 | tf_op jit(solution)/shard_map/ppermute | solution.py:42
  (115 other events, 551.8 us)
